TPU v7x, 256 devices: a whole 4x4x8 slice. The times are simulated.
256 devices in a mesh: ta: 16 (over y, x), gz: 8 (over z_hi, core), gy: 2 (over z_lo).
Axes of the slice: x: 4, y: 4, z: 8 (z_hi: 4, z_lo: 2; z = z_hi * 2 + z_lo), core: 2. Of those that a mesh axis runs over, the one named last changes fastest.
Arguments:
- current: float32 [96, 48, 2304], P('ta', 'gz', 'gy'), may hold values from -12 to 12
- kernel: float32 [96, 96, 18432], P('ta', 'gz', 'gy'), as said below
Outputs:
- potential: float32 [96, 48, 2304], P('ta', 'gz', 'gy')
Inputs may be any that keep to these rules, and one draw needn't show every extreme that they name: kernel is zero at the zero momentum (all four indices 0) and positive at every other momentum.
All inputs are finite; a program needn't handle non-finite values.
Results may differ from a plain program's by a relative error of at most 0.018.
Values may be sent and summed in bfloat16 or wider, within the bound.
No kernel may reach another device: no remote copies, remote signals or barrier semaphores. Data moves between devices by JAX's collectives and lax.ppermute only.
A program may use at most 64 MiB of HBM per device.

v0:
```python
import numpy as np

import jax
import jax.numpy as jnp
from jax import lax
from jax.experimental import pallas as pl
from jax.experimental.pallas import tpu as pltpu
from jax.sharding import PartitionSpec as P


BF = jnp.bfloat16
F32 = jnp.float32
AXES = ("ta", "gz", "gy")
PARTS = (2, 3)
SHIFTS = (0, 1, 7, 2, 6, 3, 5, 4)


def split_table(table):
    table = np.asarray(table, np.float32)
    upper = table.astype(jnp.bfloat16)
    lower = (table - upper.astype(np.float32)).astype(jnp.bfloat16)
    return np.stack([upper, lower])


def turn(numerator, period, sign):
    angle = 2.0 * np.pi * (np.asarray(numerator) % period) / period
    cosine, sine = np.cos(angle), sign * np.sin(angle)
    return np.stack([np.stack([cosine, -sine]), np.stack([sine, cosine])])


def first_forward():
    x = np.arange(48)
    i = np.arange(25)
    parts = turn(x[:, None] * i[None, :], 96, -1.0)[:, 0]
    table = np.zeros((8, 48, 5, 128))
    for y in range(8):
        block = parts.reshape(2, 48, 5, 5).transpose(1, 2, 0, 3).reshape(48, 5, 10)
        table[y, :, :, y * 10 : y * 10 + 10] = block
    return split_table(table.reshape(384, 640))


def second_forward():
    y = np.arange(48)
    out = np.zeros((8, 6, 128, 2, 64))
    for g in range(8):
        q = 12 * g + np.arange(12)
        parts = turn(y[:, None] * q[None, :], 96, -1.0)
        for i in range(5):
            for inp in range(2):
                for r in range(8):
                    out[g, :, r * 10 + inp * 5 + i, :, i * 12 : i * 12 + 12] = parts[
                        :, inp, r::8
                    ].transpose(1, 0, 2)
    table = split_table(out.reshape(8, 768, 128))
    return np.concatenate([table[0], table[1]], axis=2)


def third_forward():
    w = np.arange(96)
    z = np.arange(48)
    parts = turn(w[:, None] * z[None, :], 96, -1.0)
    table = np.zeros((96, 2, 2, 8, 8))
    table[..., :6] = parts.transpose(2, 0, 1, 3).reshape(96, 2, 2, 8, 6)
    return split_table(table.reshape(192, 128))


def time_forward():
    k = np.arange(192)
    t = np.arange(96)
    parts = turn(k[:, None] * t[None, :], 192, -1.0)
    parts = parts.transpose(0, 2, 3, 1).reshape(2, 192, 16, 6, 2).transpose(0, 1, 2, 4, 3)
    table = np.zeros((4, 2, 192, 16, 2, 8))
    table[0, ..., :6] = parts
    for s in range(3):
        table[1 + s, ..., 6:8] = parts[..., 2 * s : 2 * s + 2]
    return split_table(table.reshape(4, 384, 256))


def time_inverse():
    k = np.arange(192)
    t = np.arange(96)
    parts = turn(t[:, None] * k[None, :], 192, 1.0) / 192.0
    parts = parts.reshape(2, 2, 16, 6, 192).transpose(2, 0, 3, 1, 4)
    table = np.zeros((4, 16, 2, 8, 2, 192))
    table[0, :, :, :6] = parts
    for s in range(3):
        table[1 + s, :, :, 6:8] = parts[:, :, 2 * s : 2 * s + 2]
    return split_table(table.reshape(4, 256, 384))


def third_inverse():
    w = np.arange(96)
    z = np.arange(48)
    parts = turn(z[:, None] * w[None, :], 96, 1.0) / 96.0
    parts = parts.reshape(2, 2, 8, 6, 96).transpose(2, 0, 3, 4, 1)
    table = np.zeros((4, 8, 2, 8, 96, 2))
    table[0, :, :, :6] = parts
    for s in range(3):
        table[1 + s, :, :, 6:8] = parts[:, :, 2 * s : 2 * s + 2]
    return split_table(table.reshape(4, 128, 192))


def second_inverse():
    q = np.arange(96)
    y = np.arange(48)
    parts = turn(q[:, None] * y[None, :], 96, 1.0) / 96.0
    parts = parts.reshape(2, 2, 8, 12, 6, 8)
    table = np.zeros((8, 2, 64, 6, 128))
    for i in range(5):
        for r in range(8):
            for out in range(2):
                table[:, :, i * 12 : i * 12 + 12, :, r * 10 + out * 5 + i] = parts[
                    out, :, :, :, :, r
                ].transpose(1, 0, 2, 3)
    return split_table(table.reshape(1024, 768))


def first_inverse():
    i = np.arange(25)
    x = np.arange(48)
    parts = turn(i[:, None] * x[None, :], 96, 1.0)[0] / 96.0
    table = np.zeros((5, 128, 8, 48))
    for r in range(8):
        for inp in range(2):
            table[:, r * 10 + inp * 5 : r * 10 + inp * 5 + 5, r] = parts[inp].reshape(5, 5, 48)
    return split_table(table.reshape(640, 384))


def mirror_tables():
    flip = np.zeros((192, 192))
    flip[np.arange(192), (-np.arange(192)) % 192] = 1.0
    order = np.zeros((256, 256))
    for group in range(4):
        for i in range(5):
            for q in range(12):
                row = group * 64 + i * 12
                order[row + q, row + (12 - q) % 12] = 1.0
    return flip.astype(jnp.bfloat16), order.astype(jnp.bfloat16), np.eye(192).astype(jnp.bfloat16)


def dot(left, right):
    return lax.dot_general(left, right, (((1,), (0,)), ((), ())), preferred_element_type=F32)


def dot_rows(left, right):
    return lax.dot_general(left, right, (((1,), (1,)), ((), ())), preferred_element_type=F32)


def low_half(shape):
    return lax.broadcasted_iota(jnp.int32, shape, 1) % 128 < 64


def swap_half(values):
    return pltpu.roll(values, 64, 1)


def call(kernel, out_shape, scratch=(), in_specs=None, grid=(), vmem=14, flops=10**8, moved=4 * 10**6):
    placed = {} if in_specs is None else {"in_specs": in_specs}
    return pl.pallas_call(
        kernel,
        out_shape=out_shape,
        **placed,
        grid=grid,
        scratch_shapes=list(scratch),
        compiler_params=pltpu.CompilerParams(vmem_limit_bytes=vmem * 2**20),
        cost_estimate=pl.CostEstimate(flops=flops, bytes_accessed=moved, transcendentals=0),
    )


def vmem_spec():
    return pl.BlockSpec(memory_space=pltpu.VMEM)


def smem_spec():
    return pl.BlockSpec(memory_space=pltpu.SMEM)


def raw_kernel(current_ref, out_ref, work):
    work[...] = jnp.zeros_like(work)
    for t in range(6):
        work[8 * t : 8 * t + 6, :] = current_ref[t]
    out_ref[...] = work[...].astype(BF)


def part_of(plane):
    for part, count in enumerate(PARTS):
        if plane < count:
            return part, plane
        plane -= count


def weight_send_kernel(kernel_ref, *refs):
    plane_ref, line_ref, corner_ref, work, rows = refs[len(PARTS) :]
    rows[...] = jnp.zeros_like(rows)
    for w in range(6):
        for c in range(4):
            piece = kernel_ref[w, :, 1152 * c : 1152 * (c + 1)]
            work[12 * c : 12 * c + 12, :] = piece
            rows[4 * w + c : 4 * w + c + 1, :] = piece[0:1]
        if w == 0:
            plane_ref[...] = work[...].astype(BF)
        else:
            part, place = part_of(w - 1)
            refs[part][place] = work[...].astype(BF)
    line_ref[...] = rows[4:36, :].astype(BF)
    corner_ref[...] = rows[0:16, :].astype(BF)


def weight_own_kernel(kernel_ref, eye_ref, out_ref, work):
    eye = eye_ref[...]
    work[...] = jnp.zeros_like(work)
    for w in range(6):
        for i in range(25):
            piece = kernel_ref[w, :, 192 * i : 192 * (i + 1)]
            row = 64 * (i // 5) + 12 * (i % 5)
            if i < 20:
                work[w, row : row + 12, :] = piece
            else:
                row = 64 * (w // 2) + 12 * (i % 5)
                work[6 + w % 2, row : row + 12, :] = piece
    for v in range(8):
        values = work[v]
        upper = values.astype(BF)
        lower = (values - upper.astype(F32)).astype(BF)
        out_ref[v] = dot_rows(eye, upper) + dot_rows(eye, lower)


def weight_pair_kernel(own_ref, *refs):
    plane_ref, line_ref, corner_ref, flip_ref, order_ref, out_ref, work, held, rows = refs[
        len(PARTS) :
    ]
    flip, order = flip_ref[...], order_ref[...]
    work[...] = jnp.zeros_like(work)
    rows[0:16, :] = corner_ref[...].astype(F32)
    rows[16:48, :] = line_ref[...].astype(F32)
    for w in range(6):
        if w == 0:
            held[...] = plane_ref[...].astype(F32)
            first = 0
        else:
            part, place = part_of(5 - w)
            held[...] = refs[part][place].astype(F32)
            first = 16 + 4 * (5 - w)
        for i in range(1, 24):
            c, p = (24 - i) // 6, (24 - i) % 6
            piece = held[12 * c : 12 * c + 12, 192 * p : 192 * (p + 1)]
            line = rows[first + c : first + c + 1, 192 * p : 192 * (p + 1)]
            if i < 20:
                v, row = w, 64 * (i // 5) + 12 * (i % 5)
            else:
                v, row = 6 + w % 2, 64 * (w // 2) + 12 * (i % 5)
            work[v, row : row + 12, :] = piece
            work[v, row : row + 1, :] = line
    for v in range(8):
        turned = dot(order, work[v].astype(BF)).astype(BF)
        out_ref[v] = own_ref[v] + dot_rows(flip, turned)


def put_rows(work, row, count, values):
    work[0, pl.ds(row, count, stride=8), :] = values[:, :128]
    work[1, pl.ds(row, count, stride=8), :] = values[:, 128:]


def get_rows(work, row, count):
    halves = [work[n, pl.ds(row, count, stride=8), :] for n in range(2)]
    return jnp.concatenate(halves, axis=1)


def forward_kernel(info_ref, *refs):
    blocks = refs[:16]
    ta_ref, tb_ref, t3_ref, out_ref, raw, half, work = refs[16:]
    place, core = info_ref[0], info_ref[1]
    for n in range(16):
        spot = lax.rem(place + SHIFTS[n // 2], 8)
        side = lax.rem(spot, 2)
        plane = (spot // 2) * 2 + (core if n % 2 == 0 else 1 - core)
        for y in range(3):
            raw[side * 3 + y, plane] = blocks[n][:, 384 * y : 384 * (y + 1)]
    for y in range(6):
        rows = raw[y].reshape(384, 384)
        half[y] = (dot(rows, ta_ref[0]) + dot(rows, ta_ref[1])).astype(BF)
    seconds = []
    for ig in range(5):
        merged = jnp.concatenate([half[y, :, 128 * ig : 128 * (ig + 1)] for y in range(6)], axis=1)
        both = dot(merged, tb_ref[...])
        seconds.append(both[:, :128] + both[:, 128:])
    low = low_half((384, 128))
    real_main, imag_main = [], []
    for pair in range(2):
        left, right = seconds[2 * pair], seconds[2 * pair + 1]
        real_main.append(jnp.where(low, left, swap_half(right)))
        imag_main.append(jnp.where(low, swap_half(left), right))
    real_main = jnp.concatenate(real_main, axis=1).reshape(8, 6, 8, 256)
    imag_main = jnp.concatenate(imag_main, axis=1).reshape(8, 6, 8, 256)
    last = seconds[4].reshape(8, 6, 8, 128)
    turned = swap_half(seconds[4]).reshape(8, 6, 8, 128)
    low = low_half((64, 128))

    def finish(row, real_part, imag_part):
        merged = jnp.concatenate([real_part, imag_part], axis=0).astype(BF)
        put_rows(work, row, 192, dot(t3_ref[0], merged) + dot(t3_ref[1], merged))

    for t in range(6):
        finish(t, real_main[:, t].reshape(64, 256), imag_main[:, t].reshape(64, 256))
    for e in range(2):
        plain = [last[:, e + 2 * s].reshape(64, 128) for s in range(3)]
        moved = [turned[:, e + 2 * s].reshape(64, 128) for s in range(3)]
        real_part = [jnp.where(low, plain[0], moved[1]), jnp.where(low, plain[2], 0.0)]
        imag_part = [jnp.where(low, moved[0], plain[1]), jnp.where(low, moved[2], 0.0)]
        finish(6 + e, jnp.concatenate(real_part, axis=1), jnp.concatenate(imag_part, axis=1))
    merged = jnp.concatenate([work[0], work[1]], axis=1)
    out_ref[...] = merged.reshape(16, 6, 16, 256).astype(BF)


def gather_groups(pieces):
    pieces = pieces + [jnp.zeros_like(pieces[0])]
    return jnp.concatenate(pieces, axis=1)


def time_kernel(in_ref, weight_ref, forward_ref, inverse_ref, out_ref):
    def weighted(values, v):
        weight = weight_ref[v]
        return (values * jnp.concatenate([weight, weight], axis=0)).astype(BF)

    def forward(rows, n):
        return dot(forward_ref[0, n], rows) + dot(forward_ref[1, n], rows)

    def inverse(rows, n):
        return dot(inverse_ref[0, n], rows) + dot(inverse_ref[1, n], rows)

    loaded = [in_ref[:, w].reshape(256, 256) for w in range(6)]
    for e in range(2):
        total = None
        for s in range(3):
            rows = gather_groups([loaded[2 * r + e][:, 64 * s : 64 * (s + 1)] for r in range(3)])
            term = forward(rows, 1 + s)
            total = term if total is None else total + term
        spectrum = weighted(total, 6 + e)
        tails = [inverse(spectrum, 1 + s) for s in range(3)]
        for r in range(3):
            w = 2 * r + e
            values = inverse(weighted(forward(loaded[w], 0), w), 0)
            values = values + gather_groups([tail[:, 64 * r : 64 * (r + 1)] for tail in tails])
            out_ref[:, w] = values.astype(BF).reshape(16, 16, 256)


def third_kernel(in_ref, table_ref, out_ref, work):
    values = in_ref[...].astype(F32).reshape(1536, 256)
    work[0] = values[:, :128]
    work[1] = values[:, 128:]

    def inverse(rows, n):
        return dot(table_ref[0, n], rows) + dot(table_ref[1, n], rows)

    def load(row):
        return get_rows(work, row, 192).astype(BF)

    for e in range(2):
        rows = load(6 + e)
        tails = [inverse(rows, 1 + s) for s in range(3)]
        for r in range(3):
            t = 2 * r + e
            values = inverse(load(t), 0)
            values = values + gather_groups([tail[:, 64 * r : 64 * (r + 1)] for tail in tails])
            out_ref[:, t] = values.astype(BF).reshape(8, 16, 256)


def last_kernel(info_ref, in_ref, tb_ref, ta_ref, sign_ref, own_ref, send_ref, work, spare, both):
    side = info_ref[2]
    values = in_ref[...].astype(F32).reshape(768, 256)
    work[0] = values[:, :128]
    work[1] = values[:, 128:]
    spare[...] = jnp.zeros_like(spare)
    for e in range(2):
        rows = get_rows(work, 6 + e, 96)
        spare[pl.ds(e, 96, stride=8), :] = rows[:, :128]
        spare[pl.ds(2 + e, 96, stride=8), :] = swap_half(rows[:, :128])
        spare[pl.ds(4 + e, 96, stride=8), :] = rows[:, 128:]
    low = low_half((48, 128))
    groups = [[] for _ in range(5)]
    shaped = values.reshape(8, 6, 2, 8, 256)
    shaped_spare = spare[...].reshape(8, 6, 2, 8, 128)
    for g in range(8):
        real_part = shaped[g, :, 0].reshape(48, 256)
        imag_part = shaped[g, :, 1].reshape(48, 256)
        for pair in range(2):
            real_tile = real_part[:, 128 * pair : 128 * (pair + 1)]
            imag_tile = imag_part[:, 128 * pair : 128 * (pair + 1)]
            groups[2 * pair].append(jnp.where(low, real_tile, swap_half(imag_tile)))
            groups[2 * pair + 1].append(jnp.where(low, swap_half(real_tile), imag_tile))
        real_tile = shaped_spare[g, :, 0].reshape(48, 128)
        imag_tile = shaped_spare[g, :, 1].reshape(48, 128)
        groups[4].append(jnp.where(low, real_tile, swap_half(imag_tile)))
    rows = jnp.concatenate([jnp.concatenate(group, axis=1) for group in groups], axis=0).astype(BF)
    half = (dot(rows, tb_ref[0]) + dot(rows, tb_ref[1])).astype(BF)
    rows = jnp.concatenate(
        [
            jnp.concatenate(
                [half[48 * ig : 48 * (ig + 1), 128 * y : 128 * (y + 1)] for ig in range(5)], axis=1
            )
            for y in range(6)
        ],
        axis=0,
    )
    result = (dot(rows, ta_ref[0]) + dot(rows, ta_ref[1])) * sign_ref[...]
    for y in range(6):
        both[y // 3, :, 384 * (y % 3) : 384 * (y % 3 + 1)] = result[48 * y : 48 * (y + 1)]
    own = both[side]
    for t in range(6):
        own_ref[t] = own[8 * t : 8 * t + 6]
    send_ref[...] = both[1 - side].astype(BF)


def sum_kernel(own_ref, other_ref, out_ref):
    other = other_ref[...].astype(F32)
    for t in range(6):
        out_ref[t] = own_ref[t] + other[8 * t : 8 * t + 6]


def device_of(a, z, c):
    return (a * 8 + (z // 2) * 2 + c) * 2 + z % 2


def column_pairs(shift, flip):
    return [
        (device_of(a, (z + shift) % 8, c ^ flip), device_of(a, z, c))
        for a in range(16)
        for z in range(8)
        for c in range(2)
    ]


def mirror_pairs(a_from, g_from):
    return [
        ((((a_from - a) % 16) * 8 + (g_from - g) % 8) * 2 + 1 - h, (a * 8 + g) * 2 + h)
        for a in range(16)
        for g in range(8)
        for h in range(2)
    ]


def gather_column(block):
    def receive(values, shift, flip=0):
        return lax.ppermute(values, AXES, column_pairs(shift, flip))

    held = {0: block}
    for shift in (1, 7, 2, 6):
        held[shift] = receive(block, shift)
    held[3] = receive(held[2], 1)
    held[5] = receive(held[6], 7)
    held[4] = receive(held[2], 2)
    blocks = []
    for shift in SHIFTS:
        blocks += [held[shift], receive(held[shift], 0, 1)]
    return blocks


def shape(dims, dtype):
    return jax.ShapeDtypeStruct(dims, dtype)


def body(current, kernel):
    g = lax.axis_index("gz")
    h = lax.axis_index("gy")
    info = jnp.stack([(g // 2) * 2 + h, g % 2, h, 0]).astype(jnp.int32)
    parity = jnp.arange(384) % 2
    sign = jnp.where((parity == 1) & (h == 1), -1.0, 1.0).astype(F32)
    flip, order, eye = mirror_tables()

    block = call(raw_kernel, shape((48, 1152), BF), [pltpu.VMEM((48, 1152), F32)], vmem=8)(current)
    blocks = gather_column(block)

    sent = call(
        weight_send_kernel,
        [shape((n, 48, 1152), BF) for n in PARTS]
        + [shape((48, 1152), BF), shape((32, 1152), BF), shape((16, 1152), BF)],
        [pltpu.VMEM((48, 1152), F32), pltpu.VMEM((40, 1152), F32)],
        in_specs=[pl.BlockSpec((6, 12, 4608), lambda n: (0, 0, 1))],
        grid=(1,),
        vmem=16,
    )(kernel)
    places = ((15, 7),) * len(PARTS) + ((16, 7), (15, 8), (16, 8))
    arrived = [lax.ppermute(s, AXES, mirror_pairs(*place)) for s, place in zip(sent, places)]
    own_weight = call(
        weight_own_kernel,
        shape((8, 192, 256), F32),
        [pltpu.VMEM((8, 256, 192), F32)],
        in_specs=[pl.BlockSpec((6, 12, 4864), lambda n: (0, 0, 0)), vmem_spec()],
        grid=(1,),
        vmem=24,
    )(kernel, jnp.asarray(eye))

    ta = jnp.asarray(first_forward()) * sign.astype(BF)[None, :, None]
    tb = lax.dynamic_index_in_dim(jnp.asarray(second_forward()), g, 0, keepdims=False)
    values = call(
        forward_kernel,
        shape((16, 6, 16, 256), BF),
        [
            pltpu.VMEM((6, 8, 48, 384), BF),
            pltpu.VMEM((6, 384, 640), BF),
            pltpu.VMEM((2, 1536, 128), F32),
        ],
        in_specs=[smem_spec()] + [vmem_spec()] * 19,
    )(info, *blocks, ta, tb, jnp.asarray(third_forward()))
    values = lax.all_to_all(values, "ta", split_axis=0, concat_axis=0, tiled=True)

    weight = call(
        weight_pair_kernel,
        shape((8, 192, 256), F32),
        [
            pltpu.VMEM((8, 256, 192), F32),
            pltpu.VMEM((48, 1152), F32),
            pltpu.VMEM((48, 1152), F32),
        ],
        vmem=24,
    )(own_weight, *arrived, jnp.asarray(flip), jnp.asarray(order))
    values = call(time_kernel, shape((16, 6, 16, 256), BF))(
        values, weight, jnp.asarray(time_forward()), jnp.asarray(time_inverse())
    )
    values = lax.all_to_all(values, "ta", split_axis=0, concat_axis=0, tiled=True)
    values = call(third_kernel, shape((8, 6, 16, 256), BF), [pltpu.VMEM((2, 1536, 128), F32)])(
        values, jnp.asarray(third_inverse())
    )
    values = lax.all_to_all(values, "gz", split_axis=0, concat_axis=0, tiled=True)
    own, send = call(
        last_kernel,
        [shape((6, 6, 1152), F32), shape((48, 1152), BF)],
        [
            pltpu.VMEM((2, 768, 128), F32),
            pltpu.VMEM((768, 128), F32),
            pltpu.VMEM((2, 48, 1152), F32),
        ],
        in_specs=[smem_spec()] + [vmem_spec()] * 4,
    )(info, values, jnp.asarray(second_inverse()), jnp.asarray(first_inverse()), sign[None, :])
    other = lax.ppermute(send, "gy", [(0, 1), (1, 0)])
    return call(sum_kernel, shape((6, 6, 1152), F32), vmem=8)(own, other)


def solution(mesh):
    specs = P("ta", "gz", "gy")
    return jax.shard_map(
        body, mesh=mesh, in_specs=(specs, specs), out_specs=specs, check_vma=False
    )
```

profile of v0, /device:TPU:32, one launch (start us, length us, event | category | flops | bytes accessed | tf_op | source)
XLA Modules:
  0.0 143.3 jit_solution(13244466458280831080)
XLA Ops:
  1.6 5.4 %collective-permute-start.5 = (bf16[48,1152]{1,0:T(8,128)(2,1)}, bf16[48,1152]{1,0:T(8,128)(2,1)}, u32[]{:S(2)}, u32[]{:S(2)}) collective-permute-start(bf16[48,1152]{1,0:T(8,128)(2,1)} %shard_map.127.refs_0_), channel_id=1, source_target_pairs={{4,0},{6,2},{5,1},{7,3},{8,4},{10,6},{9,5},{11,7},{12,8},{14,10},{... | collective-permute-start | bytes 331784 | tf_op jit(solution)/shard_map/ppermute | solution.py:444
  9.1 2.3 %broadcast_multiply_fusion.refs_16_ = bf16[2,384,640]{2,1,0:T(8,128)(2,1)} fusion(bf16[2,384,640]{2,1,0:T(8,128)(2,1)} %constant.80.clone, bf16[384]{0:T(512)(128)(2,1)S(1)} %select_convert_fusion), kind=kLoop, calls=%fused_computation | loop fusion | flops 491520 | bytes 1966848 | tf_op jit(solution)/shard_map/mul | solution.py:493
  11.4 2.7 %collective-permute-start.9 = (bf16[48,1152]{1,0:T(8,128)(2,1)}, bf16[48,1152]{1,0:T(8,128)(2,1)S(1)}, u32[]{:S(2)}, u32[]{:S(2)}) collective-permute-start(bf16[48,1152]{1,0:T(8,128)(2,1)} %collective-permute-done.5.refs_6_), channel_id=1, source_target_pairs={{1,0},{3,2},{4,1},{6,3},{5,4},{7,6},{8,5},{10,7},{9,8},{11,10},{12... | collective-permute-start | bytes 331784 | tf_op jit(solution)/shard_map/ppermute | solution.py:444
  14.1 2.5 %collective-permute-done.7.refs_8_ = bf16[48,1152]{1,0:T(8,128)(2,1)} collective-permute-done((bf16[48,1152]{1,0:T(8,128)(2,1)}, bf16[48,1152]{1,0:T(8,128)(2,1)}, u32[]{:S(2)}, u32[]{:S(2)}) %collective-permute-start.7) | collective-permute-done | bytes 110624 | tf_op jit(solution)/shard_map/ppermute | solution.py:444
  16.6 1.8 %collective-permute-start.13 = (bf16[48,1152]{1,0:T(8,128)(2,1)}, bf16[48,1152]{1,0:T(8,128)(2,1)S(1)}, u32[]{:S(2)}, u32[]{:S(2)}) collective-permute-start(bf16[48,1152]{1,0:T(8,128)(2,1)} %collective-permute-done.5.refs_6_), channel_id=1, source_target_pairs={{4,0},{6,2},{5,1},{7,3},{8,4},{10,6},{9,5},{11,7},{12,8},{14,10},{... | collective-permute-start | bytes 331784 | tf_op jit(solution)/shard_map/ppermute | solution.py:444
  21.1 1.7 %collective-permute-done.13.refs_14_ = bf16[48,1152]{1,0:T(8,128)(2,1)S(1)} collective-permute-done((bf16[48,1152]{1,0:T(8,128)(2,1)}, bf16[48,1152]{1,0:T(8,128)(2,1)S(1)}, u32[]{:S(2)}, u32[]{:S(2)}) %collective-permute-start.13) | collective-permute-done | bytes 110624 | tf_op jit(solution)/shard_map/ppermute | solution.py:444
  22.8 1.3 collective-permute-done.11.refs_12_
  25.9 1.2 copy-done.1
  28.0 6.3 %shard_map.128 = bf16[16,6,16,256]{3,2,1,0:T(8,128)(2,1)S(1)} custom-call(s32[4]{0:T(128)S(1)} %pad_add_fusion.info_ref, bf16[48,1152]{1,0:T(8,128)(2,1)} %shard_map.127.refs_0_, bf16[48,1152]{1,0:T(8,128)(2,1)} %collective-permute-done.refs_1_, bf16[48,1152]{1,0:T(8,128)(2,1)} %collective-permute-done.1.refs_2_, ...), custom_call_target="tpu_custom_call" | custom-call | flops 100000000 | bytes 4000000 | tf_op jit(solution)/shard_map/pallas_call | solution.py:495
  35.3 7.3 %all-to-all-start = ((bf16[16,6,16,256]{3,2,1,0:T(8,128)(2,1)}), bf16[16,6,16,256]{3,2,1,0:T(8,128)(2,1)}, u32[]{:S(2)}, u32[]{:S(2)}) async-start(bf16[16,6,16,256]{3,2,1,0:T(8,128)(2,1)} %copy-done.3), calls=%async_computation | async-start | bytes 1572864 | tf_op jit(solution)/shard_map/all_to_all | solution.py:505
  42.9 9.2 %collective-permute-start.16 = (bf16[3,48,1152]{2,1,0:T(8,128)(2,1)S(1)}, bf16[3,48,1152]{2,1,0:T(8,128)(2,1)S(1)}, u32[]{:S(2)}, u32[]{:S(2)}) collective-permute-start(bf16[3,48,1152]{2,1,0:T(8,128)(2,1)S(1)} %get-tuple-element.13), channel_id=1, source_target_pairs={{255,0},{254,1},{253,2},{252,3},{251,4},{250,5},{249,6},{248,7},{2... | collective-permute-start | bytes 995336 | tf_op jit(solution)/shard_map/ppermute | solution.py:483
  52.3 4.5 %collective-permute-start.17 = (bf16[48,1152]{1,0:T(8,128)(2,1)S(1)}, bf16[48,1152]{1,0:T(8,128)(2,1)S(1)}, u32[]{:S(2)}, u32[]{:S(2)}) collective-permute-start(bf16[48,1152]{1,0:T(8,128)(2,1)S(1)} %get-tuple-element.14), channel_id=1, source_target_pairs={{15,0},{14,1},{13,2},{12,3},{11,4},{10,5},{9,6},{8,7},{7,8},{6,9},... | collective-permute-start | bytes 331784 | tf_op jit(solution)/shard_map/ppermute | solution.py:483
  57.0 5.9 %collective-permute-start.19 = (bf16[16,1152]{1,0:T(8,128)(2,1)S(1)}, bf16[16,1152]{1,0:T(8,128)(2,1)S(1)}, u32[]{:S(2)}, u32[]{:S(2)}) collective-permute-start(bf16[16,1152]{1,0:T(8,128)(2,1)S(1)} %get-tuple-element.16), channel_id=1, source_target_pairs={{1,0},{0,1},{15,2},{14,3},{13,4},{12,5},{11,6},{10,7},{9,8},{8,9},... | collective-permute-start | bytes 110600 | tf_op jit(solution)/shard_map/ppermute | solution.py:483
  64.0 7.0 %collective-permute-done.19.refs_4_ = bf16[16,1152]{1,0:T(8,128)(2,1)S(1)} collective-permute-done((bf16[16,1152]{1,0:T(8,128)(2,1)S(1)}, bf16[16,1152]{1,0:T(8,128)(2,1)S(1)}, u32[]{:S(2)}, u32[]{:S(2)}) %collective-permute-start.19) | collective-permute-done | bytes 36896 | tf_op jit(solution)/shard_map/ppermute | solution.py:483
  71.1 1.1 shard_map.131.weight_ref
  72.3 1.4 copy-done.5
  73.7 5.6 %shard_map.132 = bf16[16,6,16,256]{3,2,1,0:T(8,128)(2,1)S(1)} custom-call(bf16[16,6,16,256]{3,2,1,0:T(8,128)(2,1)} %all-to-all-done.in_ref, f32[8,192,256]{2,1,0:T(8,128)S(1)} %shard_map.131.weight_ref, bf16[2,4,384,256]{3,2,1,0:T(8,128)(2,1)S(1)} %copy-done.4, bf16[2,4,256,384]{3,2,1,0:T(8,128)(2,1)S(1)} %copy-done.5), custom_call_target="tpu_custom_call" | custom-call | flops 100000000 | bytes 4000000 | tf_op jit(solution)/shard_map/pallas_call | solution.py:517
  79.3 19.6 %all_to_all.15.in_ref = bf16[16,6,16,256]{3,2,1,0:T(8,128)(2,1)S(1)} all-to-all(bf16[16,6,16,256]{3,2,1,0:T(8,128)(2,1)S(1)} %shard_map.132), channel_id=1, replica_groups=mesh['ta'=16,'gz'=8,'gy'=2] {'ta'}, dimensions={0} | all-to-all | bytes 1572864 | tf_op jit(solution)/shard_map/all_to_all | solution.py:520
  98.8 1.6 %shard_map.133 = bf16[8,6,16,256]{3,2,1,0:T(8,128)(2,1)} custom-call(bf16[16,6,16,256]{3,2,1,0:T(8,128)(2,1)S(1)} %all_to_all.15.in_ref, bf16[2,4,128,192]{3,2,1,0:T(8,128)(2,1)S(1)} %copy-done.7), custom_call_target="tpu_custom_call" | custom-call | flops 100000000 | bytes 4000000 | tf_op jit(solution)/shard_map/pallas_call | solution.py:521
  100.4 18.1 %all-to-all-start.2 = ((bf16[8,6,16,256]{3,2,1,0:T(8,128)(2,1)}), bf16[8,6,16,256]{3,2,1,0:T(8,128)(2,1)S(1)}, u32[]{:S(2)}, u32[]{:S(2)}) async-start(bf16[8,6,16,256]{3,2,1,0:T(8,128)(2,1)} %shard_map.133), calls=%async_computation.2 | async-start | bytes 786432 | tf_op jit(solution)/shard_map/all_to_all | solution.py:524
  118.6 15.3 %all-to-all-done.2.in_ref = bf16[8,6,16,256]{3,2,1,0:T(8,128)(2,1)S(1)} async-done(((bf16[8,6,16,256]{3,2,1,0:T(8,128)(2,1)}), bf16[8,6,16,256]{3,2,1,0:T(8,128)(2,1)S(1)}, u32[]{:S(2)}, u32[]{:S(2)}) %all-to-all-start.2) | async-done | bytes 393248 | tf_op jit(solution)/shard_map/all_to_all | solution.py:524
  133.9 1.2 copy-done.6
  135.1 2.7 %shard_map.134 = (f32[6,6,1152]{2,1,0:T(8,128)S(1)}, bf16[48,1152]{1,0:T(8,128)(2,1)S(1)}) custom-call(s32[4]{0:T(128)S(1)} %pad_add_fusion.info_ref, bf16[8,6,16,256]{3,2,1,0:T(8,128)(2,1)S(1)} %all-to-all-done.2.in_ref, bf16[2,1024,768]{2,1,0:T(8,128)(2,1)S(1)} %copy-done.2, bf16[2,640,384]{2,1,0:T(8,128)(2,1)S(1)} %copy-done.6, ...), custom_call_target="tpu_custom_call" | custom-call | flops 100000000 | bytes 4000000 | tf_op jit(solution)/shard_map/pallas_call | solution.py:525
  138.8 3.8 %collective-permute-done.20.other_ref = bf16[48,1152]{1,0:T(8,128)(2,1)S(1)} collective-permute-done((bf16[48,1152]{1,0:T(8,128)(2,1)S(1)}, bf16[48,1152]{1,0:T(8,128)(2,1)S(1)}, u32[]{:S(2)}, u32[]{:S(2)}) %collective-permute-start.20) | collective-permute-done | bytes 110624 | tf_op jit(solution)/shard_map/ppermute | solution.py:535
  (63 shorter events, 13.7 us)
Async XLA Ops:
  1.6 9.8 %collective-permute-start.5 = (bf16[48,1152]{1,0:T(8,128)(2,1)}, bf16[48,1152]{1,0:T(8,128)(2,1)}, u32[]{:S(2)}, u32[]{:S(2)}) collective-permute-start(bf16[48,1152]{1,0:T(8,128)(2,1)} %shard_map.127.refs_0_), channel_id=1, source_target_pairs={{4,0},{6,2},{5,1},{7,3},{8,4},{10,6},{9,5},{11,7},{12,8},{14,10},{... | collective-permute-start | bytes 331784 | tf_op jit(solution)/shard_map/ppermute | solution.py:444
  7.0 9.6 %collective-permute-start.7 = (bf16[48,1152]{1,0:T(8,128)(2,1)}, bf16[48,1152]{1,0:T(8,128)(2,1)}, u32[]{:S(2)}, u32[]{:S(2)}) collective-permute-start(bf16[48,1152]{1,0:T(8,128)(2,1)} %shard_map.127.refs_0_), channel_id=1, source_target_pairs={{12,0},{14,2},{13,1},{15,3},{0,4},{2,6},{1,5},{3,7},{4,8},{6,10},{... | collective-permute-start | bytes 331784 | tf_op jit(solution)/shard_map/ppermute | solution.py:444
  7.0 11.4 %collective-permute-start.1 = (bf16[48,1152]{1,0:T(8,128)(2,1)}, bf16[48,1152]{1,0:T(8,128)(2,1)}, u32[]{:S(2)}, u32[]{:S(2)}) collective-permute-start(bf16[48,1152]{1,0:T(8,128)(2,1)} %shard_map.127.refs_0_), channel_id=1, source_target_pairs={{1,0},{3,2},{4,1},{6,3},{5,4},{7,6},{8,5},{10,7},{9,8},{11,10},{12... | collective-permute-start | bytes 331784 | tf_op jit(solution)/shard_map/ppermute | solution.py:444
  8.0 10.4 %collective-permute-start.3 = (bf16[48,1152]{1,0:T(8,128)(2,1)}, bf16[48,1152]{1,0:T(8,128)(2,1)}, u32[]{:S(2)}, u32[]{:S(2)}) collective-permute-start(bf16[48,1152]{1,0:T(8,128)(2,1)} %shard_map.127.refs_0_), channel_id=1, source_target_pairs={{13,0},{15,2},{0,1},{2,3},{1,4},{3,6},{4,5},{6,7},{5,8},{7,10},{8,... | collective-permute-start | bytes 331784 | tf_op jit(solution)/shard_map/ppermute | solution.py:444
  9.1 10.5 %collective-permute-start = (bf16[48,1152]{1,0:T(8,128)(2,1)}, bf16[48,1152]{1,0:T(8,128)(2,1)}, u32[]{:S(2)}, u32[]{:S(2)}) collective-permute-start(bf16[48,1152]{1,0:T(8,128)(2,1)} %shard_map.127.refs_0_), channel_id=1, source_target_pairs={{2,0},{0,2},{3,1},{1,3},{6,4},{4,6},{7,5},{5,7},{10,8},{8,10},{11,... | collective-permute-start | bytes 331784 | tf_op jit(solution)/shard_map/ppermute | solution.py:444
  11.4 9.3 %collective-permute-start.9 = (bf16[48,1152]{1,0:T(8,128)(2,1)}, bf16[48,1152]{1,0:T(8,128)(2,1)S(1)}, u32[]{:S(2)}, u32[]{:S(2)}) collective-permute-start(bf16[48,1152]{1,0:T(8,128)(2,1)} %collective-permute-done.5.refs_6_), channel_id=1, source_target_pairs={{1,0},{3,2},{4,1},{6,3},{5,4},{7,6},{8,5},{10,7},{9,8},{11,10},{12... | collective-permute-start | bytes 331784 | tf_op jit(solution)/shard_map/ppermute | solution.py:444
  16.6 6.2 %collective-permute-start.13 = (bf16[48,1152]{1,0:T(8,128)(2,1)}, bf16[48,1152]{1,0:T(8,128)(2,1)S(1)}, u32[]{:S(2)}, u32[]{:S(2)}) collective-permute-start(bf16[48,1152]{1,0:T(8,128)(2,1)} %collective-permute-done.5.refs_6_), channel_id=1, source_target_pairs={{4,0},{6,2},{5,1},{7,3},{8,4},{10,6},{9,5},{11,7},{12,8},{14,10},{... | collective-permute-start | bytes 331784 | tf_op jit(solution)/shard_map/ppermute | solution.py:444
  18.4 5.7 %collective-permute-start.6 = (bf16[48,1152]{1,0:T(8,128)(2,1)}, bf16[48,1152]{1,0:T(8,128)(2,1)S(1)}, u32[]{:S(2)}, u32[]{:S(2)}) collective-permute-start(bf16[48,1152]{1,0:T(8,128)(2,1)} %collective-permute-done.5.refs_6_), channel_id=1, source_target_pairs={{2,0},{0,2},{3,1},{1,3},{6,4},{4,6},{7,5},{5,7},{10,8},{8,10},{11,... | collective-permute-start | bytes 331784 | tf_op jit(solution)/shard_map/ppermute | solution.py:444
  18.4 5.7 %collective-permute-start.11 = (bf16[48,1152]{1,0:T(8,128)(2,1)}, bf16[48,1152]{1,0:T(8,128)(2,1)S(1)}, u32[]{:S(2)}, u32[]{:S(2)}) collective-permute-start(bf16[48,1152]{1,0:T(8,128)(2,1)} %collective-permute-done.7.refs_8_), channel_id=1, source_target_pairs={{13,0},{15,2},{0,1},{2,3},{1,4},{3,6},{4,5},{6,7},{5,8},{7,10},{8,... | collective-permute-start | bytes 331784 | tf_op jit(solution)/shard_map/ppermute | solution.py:444
  19.5 5.1 %collective-permute-start.8 = (bf16[48,1152]{1,0:T(8,128)(2,1)}, bf16[48,1152]{1,0:T(8,128)(2,1)S(1)}, u32[]{:S(2)}, u32[]{:S(2)}) collective-permute-start(bf16[48,1152]{1,0:T(8,128)(2,1)} %collective-permute-done.7.refs_8_), channel_id=1, source_target_pairs={{2,0},{0,2},{3,1},{1,3},{6,4},{4,6},{7,5},{5,7},{10,8},{8,10},{11,... | collective-permute-start | bytes 331784 | tf_op jit(solution)/shard_map/ppermute | solution.py:444
  20.7 4.3 %collective-permute-start.2 = (bf16[48,1152]{1,0:T(8,128)(2,1)}, bf16[48,1152]{1,0:T(8,128)(2,1)S(1)}, u32[]{:S(2)}, u32[]{:S(2)}) collective-permute-start(bf16[48,1152]{1,0:T(8,128)(2,1)} %collective-permute-done.1.refs_2_), channel_id=1, source_target_pairs={{2,0},{0,2},{3,1},{1,3},{6,4},{4,6},{7,5},{5,7},{10,8},{8,10},{11,... | collective-permute-start | bytes 331784 | tf_op jit(solution)/shard_map/ppermute | solution.py:444
  22.8 2.1 %collective-permute-start.4 = (bf16[48,1152]{1,0:T(8,128)(2,1)}, bf16[48,1152]{1,0:T(8,128)(2,1)S(1)}, u32[]{:S(2)}, u32[]{:S(2)}) collective-permute-start(bf16[48,1152]{1,0:T(8,128)(2,1)} %collective-permute-done.3.refs_4_), channel_id=1, source_target_pairs={{2,0},{0,2},{3,1},{1,3},{6,4},{4,6},{7,5},{5,7},{10,8},{8,10},{11,... | collective-permute-start | bytes 331784 | tf_op jit(solution)/shard_map/ppermute | solution.py:444
  24.1 1.3 collective-permute-start.10
  24.1 1.5 %collective-permute-start.14 = (bf16[48,1152]{1,0:T(8,128)(2,1)S(1)}, bf16[48,1152]{1,0:T(8,128)(2,1)S(1)}, u32[]{:S(2)}, u32[]{:S(2)}) collective-permute-start(bf16[48,1152]{1,0:T(8,128)(2,1)S(1)} %collective-permute-done.13.refs_14_), channel_id=1, source_target_pairs={{2,0},{0,2},{3,1},{1,3},{6,4},{4,6},{7,5},{5,7},{10,8},{8,10},{11,... | collective-permute-start | bytes 331784 | tf_op jit(solution)/shard_map/ppermute | solution.py:444
  24.6 1.3 collective-permute-start.12
  35.3 37.0 %all-to-all-start = ((bf16[16,6,16,256]{3,2,1,0:T(8,128)(2,1)}), bf16[16,6,16,256]{3,2,1,0:T(8,128)(2,1)}, u32[]{:S(2)}, u32[]{:S(2)}) async-start(bf16[16,6,16,256]{3,2,1,0:T(8,128)(2,1)} %copy-done.3), calls=%async_computation | async-start | bytes 1572864 | tf_op jit(solution)/shard_map/all_to_all | solution.py:505
  42.9 28.2 %collective-permute-start.16 = (bf16[3,48,1152]{2,1,0:T(8,128)(2,1)S(1)}, bf16[3,48,1152]{2,1,0:T(8,128)(2,1)S(1)}, u32[]{:S(2)}, u32[]{:S(2)}) collective-permute-start(bf16[3,48,1152]{2,1,0:T(8,128)(2,1)S(1)} %get-tuple-element.13), channel_id=1, source_target_pairs={{255,0},{254,1},{253,2},{252,3},{251,4},{250,5},{249,6},{248,7},{2... | collective-permute-start | bytes 995336 | tf_op jit(solution)/shard_map/ppermute | solution.py:483
  52.2 18.9 %collective-permute-start.15 = (bf16[2,48,1152]{2,1,0:T(8,128)(2,1)S(1)}, bf16[2,48,1152]{2,1,0:T(8,128)(2,1)S(1)}, u32[]{:S(2)}, u32[]{:S(2)}) collective-permute-start(bf16[2,48,1152]{2,1,0:T(8,128)(2,1)S(1)} %get-tuple-element.12), channel_id=1, source_target_pairs={{255,0},{254,1},{253,2},{252,3},{251,4},{250,5},{249,6},{248,7},{2... | collective-permute-start | bytes 663560 | tf_op jit(solution)/shard_map/ppermute | solution.py:483
  52.3 18.8 %collective-permute-start.17 = (bf16[48,1152]{1,0:T(8,128)(2,1)S(1)}, bf16[48,1152]{1,0:T(8,128)(2,1)S(1)}, u32[]{:S(2)}, u32[]{:S(2)}) collective-permute-start(bf16[48,1152]{1,0:T(8,128)(2,1)S(1)} %get-tuple-element.14), channel_id=1, source_target_pairs={{15,0},{14,1},{13,2},{12,3},{11,4},{10,5},{9,6},{8,7},{7,8},{6,9},... | collective-permute-start | bytes 331784 | tf_op jit(solution)/shard_map/ppermute | solution.py:483
  56.8 14.3 %collective-permute-start.18 = (bf16[32,1152]{1,0:T(8,128)(2,1)S(1)}, bf16[32,1152]{1,0:T(8,128)(2,1)S(1)}, u32[]{:S(2)}, u32[]{:S(2)}) collective-permute-start(bf16[32,1152]{1,0:T(8,128)(2,1)S(1)} %get-tuple-element.15), channel_id=1, source_target_pairs={{241,0},{240,1},{255,2},{254,3},{253,4},{252,5},{251,6},{250,7},{2... | collective-permute-start | bytes 221192 | tf_op jit(solution)/shard_map/ppermute | solution.py:483
  57.0 14.0 %collective-permute-start.19 = (bf16[16,1152]{1,0:T(8,128)(2,1)S(1)}, bf16[16,1152]{1,0:T(8,128)(2,1)S(1)}, u32[]{:S(2)}, u32[]{:S(2)}) collective-permute-start(bf16[16,1152]{1,0:T(8,128)(2,1)S(1)} %get-tuple-element.16), channel_id=1, source_target_pairs={{1,0},{0,1},{15,2},{14,3},{13,4},{12,5},{11,6},{10,7},{9,8},{8,9},... | collective-permute-start | bytes 110600 | tf_op jit(solution)/shard_map/ppermute | solution.py:483
  79.3 54.6 %copy-start.2 = (bf16[2,1024,768]{2,1,0:T(8,128)(2,1)S(1)}, bf16[2,1024,768]{2,1,0:T(8,128)(2,1)}, u32[]{:S(2)}) copy-start(bf16[2,1024,768]{2,1,0:T(8,128)(2,1)} %constant.88.clone.tb_ref) | copy-start | bytes 9437188
  100.4 33.4 %all-to-all-start.2 = ((bf16[8,6,16,256]{3,2,1,0:T(8,128)(2,1)}), bf16[8,6,16,256]{3,2,1,0:T(8,128)(2,1)S(1)}, u32[]{:S(2)}, u32[]{:S(2)}) async-start(bf16[8,6,16,256]{3,2,1,0:T(8,128)(2,1)} %shard_map.133), calls=%async_computation.2 | async-start | bytes 786432 | tf_op jit(solution)/shard_map/all_to_all | solution.py:524
  137.8 4.8 %collective-permute-start.20 = (bf16[48,1152]{1,0:T(8,128)(2,1)S(1)}, bf16[48,1152]{1,0:T(8,128)(2,1)S(1)}, u32[]{:S(2)}, u32[]{:S(2)}) collective-permute-start(bf16[48,1152]{1,0:T(8,128)(2,1)S(1)} %get-tuple-element.18), channel_id=1, source_target_pairs={{0,1},{1,0},{2,3},{3,2},{4,5},{5,4},{6,7},{7,6},{8,9},{9,8},{10,11... | collective-permute-start | bytes 331784 | tf_op jit(solution)/shard_map/ppermute | solution.py:535
  (12 other events, 147.8 us)
where the time goes:
time: 144 us; the launch traced here: 143 us
  starting transfers between devices  60.8 us (42%)
  waiting for transfers between devices  32.7 us (23%)
  Pallas kernels  20.1 us (14%)
  blocking collectives  19.6 us (14%)
  local copies, waits for them, and re-layouts  7.6 us (5%)
  other arithmetic  2.43 us (2%)
    ppermute x5, starting transfers between devices, body(): lax.ppermute(s, AXES, mirror_pairs(*place))  19.9 us
    all_to_all x1, blocking collectives, body(): lax.all_to_all(values, 'ta', split_axis=0, concat_axis=0, tiled=True)  19.6 us
    all_to_all x1, starting transfers between devices, body(): lax.all_to_all(values, 'gz', split_axis=0, concat_axis=0, tiled=True)  18.1 us
    all_to_all x1, waiting for transfers between devices, body(): lax.all_to_all(values, 'gz', split_axis=0, concat_axis=0, tiled=True)  15.3 us
    ppermute x15, starting transfers between devices, receive(): return lax.ppermute(values, AXES, column_pairs(shift, flip))  14.4 us
    all_to_all x1, starting transfers between devices, body(): lax.all_to_all(values, 'ta', split_axis=0, concat_axis=0, tiled=True)  7.3 us
    ppermute x5, waiting for transfers between devices, body(): lax.ppermute(s, AXES, mirror_pairs(*place))  7.12 us
    unnamed x26, local copies, waits for them, and re-layouts  6.58 us
  transfers between devices with their start and end apart: 23, of which 10 were waited for; matrix products, arithmetic and copies ran while one was open for 2% of the time, Pallas kernels for 2%

commit v1 on v0

--- a/solution.py
+++ b/solution.py
@@ -11,13 +11,15 @@
 BF = jnp.bfloat16
 F32 = jnp.float32
 AXES = ("ta", "gz", "gy")
-PARTS = (2, 3)
+PARTS = (5,)
 SHIFTS = (0, 1, 7, 2, 6, 3, 5, 4)
 
 
-def split_table(table):
+def split_table(table, parts=2):
     table = np.asarray(table, np.float32)
     upper = table.astype(jnp.bfloat16)
+    if parts == 1:
+        return upper[None]
     lower = (table - upper.astype(np.float32)).astype(jnp.bfloat16)
     return np.stack([upper, lower])
 
@@ -36,7 +38,7 @@
     for y in range(8):
         block = parts.reshape(2, 48, 5, 5).transpose(1, 2, 0, 3).reshape(48, 5, 10)
         table[y, :, :, y * 10 : y * 10 + 10] = block
-    return split_table(table.reshape(384, 640))
+    return split_table(table.reshape(384, 640), 1)
 
 
 def second_forward():
@@ -73,7 +75,7 @@
     table[0, ..., :6] = parts
     for s in range(3):
         table[1 + s, ..., 6:8] = parts[..., 2 * s : 2 * s + 2]
-    return split_table(table.reshape(4, 384, 256))
+    return split_table(table.reshape(4, 384, 256), 1)
 
 
 def time_inverse():
@@ -85,7 +87,7 @@
     table[0, :, :, :6] = parts
     for s in range(3):
         table[1 + s, :, :, 6:8] = parts[:, :, 2 * s : 2 * s + 2]
-    return split_table(table.reshape(4, 256, 384))
+    return split_table(table.reshape(4, 256, 384), 1)
 
 
 def third_inverse():
@@ -112,7 +114,7 @@
                 table[:, :, i * 12 : i * 12 + 12, :, r * 10 + out * 5 + i] = parts[
                     out, :, :, :, :, r
                 ].transpose(1, 0, 2, 3)
-    return split_table(table.reshape(1024, 768))
+    return split_table(table.reshape(1024, 768), 1)
 
 
 def first_inverse():
@@ -140,6 +142,30 @@
 
 def dot(left, right):
     return lax.dot_general(left, right, (((1,), (0,)), ((), ())), preferred_element_type=F32)
+
+
+def dot_table(table_ref, rows, *place):
+    total = dot(table_ref[(0, *place)], rows)
+    for n in range(1, table_ref.shape[0]):
+        total = total + dot(table_ref[(n, *place)], rows)
+    return total
+
+
+def dot_columns(rows, table_ref):
+    total = dot(rows, table_ref[0])
+    for n in range(1, table_ref.shape[0]):
+        total = total + dot(rows, table_ref[n])
+    return total
+
+
+def start_copies(sources, targets, arrival):
+    copies = [
+        pltpu.make_async_copy(source, target, arrival.at[n])
+        for n, (source, target) in enumerate(zip(sources, targets))
+    ]
+    for copy in copies:
+        copy.start()
+    return copies
 
 
 def dot_rows(left, right):
@@ -189,8 +215,12 @@
         plane -= count
 
 
-def weight_send_kernel(kernel_ref, *refs):
-    plane_ref, line_ref, corner_ref, work, rows = refs[len(PARTS) :]
+def weight_send_kernel(source_ref, *refs):
+    refs = refs[16:]
+    plane_ref, line_ref, corner_ref, work, rows, kernel_ref, arrival = refs[len(PARTS) :]
+    copy = pltpu.make_async_copy(source_ref.at[:, :, pl.ds(4608, 4608)], kernel_ref, arrival)
+    copy.start()
+    copy.wait()
     rows[...] = jnp.zeros_like(rows)
     for w in range(6):
         for c in range(4):
@@ -202,11 +232,11 @@
         else:
             part, place = part_of(w - 1)
             refs[part][place] = work[...].astype(BF)
-    line_ref[...] = rows[4:36, :].astype(BF)
-    corner_ref[...] = rows[0:16, :].astype(BF)
-
-
-def weight_own_kernel(kernel_ref, eye_ref, out_ref, work):
+    line_ref[...] = rows[4:28, :].astype(BF)
+    corner_ref[...] = rows[0:8, :].astype(BF)
+
+
+def own_weights(kernel_ref, eye_ref, weight, work):
     eye = eye_ref[...]
     work[...] = jnp.zeros_like(work)
     for w in range(6):
@@ -222,17 +252,15 @@
         values = work[v]
         upper = values.astype(BF)
         lower = (values - upper.astype(F32)).astype(BF)
-        out_ref[v] = dot_rows(eye, upper) + dot_rows(eye, lower)
-
-
-def weight_pair_kernel(own_ref, *refs):
-    plane_ref, line_ref, corner_ref, flip_ref, order_ref, out_ref, work, held, rows = refs[
-        len(PARTS) :
-    ]
+        weight[v] = dot_rows(eye, upper) + dot_rows(eye, lower)
+
+
+def pair_weights(refs, flip_ref, order_ref, weight, work, held, rows):
+    plane_ref, line_ref, corner_ref = refs[len(PARTS) :]
     flip, order = flip_ref[...], order_ref[...]
     work[...] = jnp.zeros_like(work)
-    rows[0:16, :] = corner_ref[...].astype(F32)
-    rows[16:48, :] = line_ref[...].astype(F32)
+    rows[0:8, :] = corner_ref[...].astype(F32)
+    rows[8:32, :] = line_ref[...].astype(F32)
     for w in range(6):
         if w == 0:
             held[...] = plane_ref[...].astype(F32)
@@ -240,7 +268,7 @@
         else:
             part, place = part_of(5 - w)
             held[...] = refs[part][place].astype(F32)
-            first = 16 + 4 * (5 - w)
+            first = 8 + 4 * (5 - w)
         for i in range(1, 24):
             c, p = (24 - i) // 6, (24 - i) % 6
             piece = held[12 * c : 12 * c + 12, 192 * p : 192 * (p + 1)]
@@ -253,7 +281,7 @@
             work[v, row : row + 1, :] = line
     for v in range(8):
         turned = dot(order, work[v].astype(BF)).astype(BF)
-        out_ref[v] = own_ref[v] + dot_rows(flip, turned)
+        weight[v] = weight[v] + dot_rows(flip, turned)
 
 
 def put_rows(work, row, count, values):
@@ -266,19 +294,27 @@
     return jnp.concatenate(halves, axis=1)
 
 
-def forward_kernel(info_ref, *refs):
-    blocks = refs[:16]
-    ta_ref, tb_ref, t3_ref, out_ref, raw, half, work = refs[16:]
+def forward_kernel(info_ref, sign_ref, *refs):
+    sources = list(refs[:19])
+    sources[17] = sources[17].at[info_ref[3]]
+    out_ref, raw, half, work, blocks, ta_ref, tb_ref, t3_ref, arrival = refs[19:]
+    targets = [blocks.at[n] for n in range(16)] + [ta_ref, tb_ref, t3_ref]
+    copies = start_copies(sources, targets, arrival)
+    for copy in copies[:17]:
+        copy.wait()
     place, core = info_ref[0], info_ref[1]
     for n in range(16):
         spot = lax.rem(place + SHIFTS[n // 2], 8)
         side = lax.rem(spot, 2)
         plane = (spot // 2) * 2 + (core if n % 2 == 0 else 1 - core)
         for y in range(3):
-            raw[side * 3 + y, plane] = blocks[n][:, 384 * y : 384 * (y + 1)]
+            raw[side * 3 + y, plane] = blocks[n, :, 384 * y : 384 * (y + 1)]
     for y in range(6):
         rows = raw[y].reshape(384, 384)
-        half[y] = (dot(rows, ta_ref[0]) + dot(rows, ta_ref[1])).astype(BF)
+        rows = (rows.astype(F32) * sign_ref[...]).astype(BF)
+        half[y] = dot_columns(rows, ta_ref).astype(BF)
+    for copy in copies[17:]:
+        copy.wait()
     seconds = []
     for ig in range(5):
         merged = jnp.concatenate([half[y, :, 128 * ig : 128 * (ig + 1)] for y in range(6)], axis=1)
@@ -298,7 +334,7 @@
 
     def finish(row, real_part, imag_part):
         merged = jnp.concatenate([real_part, imag_part], axis=0).astype(BF)
-        put_rows(work, row, 192, dot(t3_ref[0], merged) + dot(t3_ref[1], merged))
+        put_rows(work, row, 192, dot_table(t3_ref, merged))
 
     for t in range(6):
         finish(t, real_main[:, t].reshape(64, 256), imag_main[:, t].reshape(64, 256))
@@ -317,16 +353,30 @@
     return jnp.concatenate(pieces, axis=1)
 
 
-def time_kernel(in_ref, weight_ref, forward_ref, inverse_ref, out_ref):
+def time_kernel(*refs):
+    count = len(PARTS) + 10
+    sources, out_ref, targets = refs[:count], refs[count], refs[count + 1 : 2 * count + 1]
+    work, held, rows, weight, arrival = refs[2 * count + 1 :]
+    sources = list(sources)
+    sources[0] = sources[0].at[:, :, pl.ds(0, 4864)]
+    copies = start_copies(sources, targets, arrival)
+    eye_ref, flip_ref, order_ref, forward_ref, inverse_ref, in_ref = targets[count - 6 :]
+    for copy in copies[: count - 3]:
+        copy.wait()
+    own_weights(targets[0], eye_ref, weight, work)
+    pair_weights(targets[1 : count - 6], flip_ref, order_ref, weight, work, held, rows)
+    for copy in copies[count - 3 :]:
+        copy.wait()
+
     def weighted(values, v):
-        weight = weight_ref[v]
-        return (values * jnp.concatenate([weight, weight], axis=0)).astype(BF)
+        part = weight[v]
+        return (values * jnp.concatenate([part, part], axis=0)).astype(BF)
 
     def forward(rows, n):
-        return dot(forward_ref[0, n], rows) + dot(forward_ref[1, n], rows)
+        return dot_table(forward_ref, rows, n)
 
     def inverse(rows, n):
-        return dot(inverse_ref[0, n], rows) + dot(inverse_ref[1, n], rows)
+        return dot_table(inverse_ref, rows, n)
 
     loaded = [in_ref[:, w].reshape(256, 256) for w in range(6)]
     for e in range(2):
@@ -365,7 +415,11 @@
             out_ref[:, t] = values.astype(BF).reshape(8, 16, 256)
 
 
-def last_kernel(info_ref, in_ref, tb_ref, ta_ref, sign_ref, own_ref, send_ref, work, spare, both):
+def last_kernel(
+    info_ref, in_ref, tb_source, ta_source, sign_ref, own_ref, send_ref, work, spare, both,
+    tb_ref, ta_ref, arrival
+):
+    copies = start_copies((tb_source, ta_source), (tb_ref, ta_ref), arrival)
     side = info_ref[2]
     values = in_ref[...].astype(F32).reshape(768, 256)
     work[0] = values[:, :128]
@@ -392,7 +446,9 @@
         imag_tile = shaped_spare[g, :, 1].reshape(48, 128)
         groups[4].append(jnp.where(low, real_tile, swap_half(imag_tile)))
     rows = jnp.concatenate([jnp.concatenate(group, axis=1) for group in groups], axis=0).astype(BF)
-    half = (dot(rows, tb_ref[0]) + dot(rows, tb_ref[1])).astype(BF)
+    for copy in copies:
+        copy.wait()
+    half = dot_columns(rows, tb_ref).astype(BF)
     rows = jnp.concatenate(
         [
             jnp.concatenate(
@@ -402,7 +458,7 @@
         ],
         axis=0,
     )
-    result = (dot(rows, ta_ref[0]) + dot(rows, ta_ref[1])) * sign_ref[...]
+    result = dot_columns(rows, ta_ref) * sign_ref[...]
     for y in range(6):
         both[y // 3, :, 384 * (y % 3) : 384 * (y % 3 + 1)] = result[48 * y : 48 * (y + 1)]
     own = both[side]
@@ -462,61 +518,71 @@
 def body(current, kernel):
     g = lax.axis_index("gz")
     h = lax.axis_index("gy")
-    info = jnp.stack([(g // 2) * 2 + h, g % 2, h, 0]).astype(jnp.int32)
+    info = jnp.stack([(g // 2) * 2 + h, g % 2, h, g]).astype(jnp.int32)
     parity = jnp.arange(384) % 2
     sign = jnp.where((parity == 1) & (h == 1), -1.0, 1.0).astype(F32)
     flip, order, eye = mirror_tables()
 
+    anywhere = pl.BlockSpec(memory_space=pl.ANY)
     block = call(raw_kernel, shape((48, 1152), BF), [pltpu.VMEM((48, 1152), F32)], vmem=8)(current)
     blocks = gather_column(block)
 
     sent = call(
         weight_send_kernel,
         [shape((n, 48, 1152), BF) for n in PARTS]
-        + [shape((48, 1152), BF), shape((32, 1152), BF), shape((16, 1152), BF)],
-        [pltpu.VMEM((48, 1152), F32), pltpu.VMEM((40, 1152), F32)],
-        in_specs=[pl.BlockSpec((6, 12, 4608), lambda n: (0, 0, 1))],
-        grid=(1,),
-        vmem=16,
-    )(kernel)
+        + [shape((48, 1152), BF), shape((24, 1152), BF), shape((8, 1152), BF)],
+        [pltpu.VMEM((48, 1152), F32), pltpu.VMEM((32, 1152), F32)]
+        + [pltpu.VMEM((6, 12, 4608), F32), pltpu.SemaphoreType.DMA],
+        in_specs=[anywhere] * 17,
+        vmem=59,
+    )(kernel, *blocks)
     places = ((15, 7),) * len(PARTS) + ((16, 7), (15, 8), (16, 8))
     arrived = [lax.ppermute(s, AXES, mirror_pairs(*place)) for s, place in zip(sent, places)]
-    own_weight = call(
-        weight_own_kernel,
-        shape((8, 192, 256), F32),
-        [pltpu.VMEM((8, 256, 192), F32)],
-        in_specs=[pl.BlockSpec((6, 12, 4864), lambda n: (0, 0, 0)), vmem_spec()],
-        grid=(1,),
-        vmem=24,
-    )(kernel, jnp.asarray(eye))
-
-    ta = jnp.asarray(first_forward()) * sign.astype(BF)[None, :, None]
-    tb = lax.dynamic_index_in_dim(jnp.asarray(second_forward()), g, 0, keepdims=False)
+    def spread(*operands):
+        values = call(
+            forward_kernel,
+            shape((16, 6, 16, 256), BF),
+            [
+                pltpu.VMEM((6, 8, 48, 384), BF),
+                pltpu.VMEM((6, 384, 640), BF),
+                pltpu.VMEM((2, 1536, 128), F32),
+                pltpu.VMEM((16, 48, 1152), BF),
+                pltpu.VMEM((1, 384, 640), BF),
+                pltpu.VMEM((768, 256), BF),
+                pltpu.VMEM((2, 192, 128), BF),
+                pltpu.SemaphoreType.DMA((19,)),
+            ],
+            in_specs=[smem_spec(), vmem_spec()] + [anywhere] * 19,
+            vmem=59,
+        )(*operands)
+        return lax.all_to_all(values, "ta", split_axis=0, concat_axis=0, tiled=True)
+
+    values = lax.cond(
+        g < lax.axis_size("gz"),
+        spread,
+        lambda *operands: jnp.zeros((16, 6, 16, 256), BF),
+        info, sign[None, :], *blocks, jnp.asarray(first_forward()), jnp.asarray(second_forward()),
+        jnp.asarray(third_forward()),
+    )
+    operands = (
+        kernel, *arrived, jnp.asarray(eye), jnp.asarray(flip), jnp.asarray(order),
+        jnp.asarray(time_forward()), jnp.asarray(time_inverse()), values
+    )
     values = call(
-        forward_kernel,
+        time_kernel,
         shape((16, 6, 16, 256), BF),
-        [
-            pltpu.VMEM((6, 8, 48, 384), BF),
-            pltpu.VMEM((6, 384, 640), BF),
-            pltpu.VMEM((2, 1536, 128), F32),
-        ],
-        in_specs=[smem_spec()] + [vmem_spec()] * 19,
-    )(info, *blocks, ta, tb, jnp.asarray(third_forward()))
-    values = lax.all_to_all(values, "ta", split_axis=0, concat_axis=0, tiled=True)
-
-    weight = call(
-        weight_pair_kernel,
-        shape((8, 192, 256), F32),
-        [
+        [pltpu.VMEM((6, 12, 4864), F32)]
+        + [pltpu.VMEM(operand.shape, operand.dtype) for operand in operands[1:]]
+        + [
             pltpu.VMEM((8, 256, 192), F32),
             pltpu.VMEM((48, 1152), F32),
-            pltpu.VMEM((48, 1152), F32),
+            pltpu.VMEM((32, 1152), F32),
+            pltpu.VMEM((8, 192, 256), F32),
+            pltpu.SemaphoreType.DMA((len(operands),)),
         ],
-        vmem=24,
-    )(own_weight, *arrived, jnp.asarray(flip), jnp.asarray(order))
-    values = call(time_kernel, shape((16, 6, 16, 256), BF))(
-        values, weight, jnp.asarray(time_forward()), jnp.asarray(time_inverse())
-    )
+        in_specs=[anywhere] * len(operands),
+        vmem=59,
+    )(*operands)
     values = lax.all_to_all(values, "ta", split_axis=0, concat_axis=0, tiled=True)
     values = call(third_kernel, shape((8, 6, 16, 256), BF), [pltpu.VMEM((2, 1536, 128), F32)])(
         values, jnp.asarray(third_inverse())
@@ -529,8 +595,11 @@
             pltpu.VMEM((2, 768, 128), F32),
             pltpu.VMEM((768, 128), F32),
             pltpu.VMEM((2, 48, 1152), F32),
+            pltpu.VMEM((1, 1024, 768), BF),
+            pltpu.VMEM((2, 640, 384), BF),
+            pltpu.SemaphoreType.DMA((2,)),
         ],
-        in_specs=[smem_spec()] + [vmem_spec()] * 4,
+        in_specs=[smem_spec(), vmem_spec(), anywhere, anywhere, vmem_spec()],
     )(info, values, jnp.asarray(second_inverse()), jnp.asarray(first_inverse()), sign[None, :])
     other = lax.ppermute(send, "gy", [(0, 1), (1, 0)])
     return call(sum_kernel, shape((6, 6, 1152), F32), vmem=8)(own, other)

time: 144 us -> 134 us (0.931)
  blocking collectives: 19.6 us -> 63.4 us
  starting transfers between devices: 60.8 us -> 31.5 us
  waiting for transfers between devices: 32.7 us -> 12.5 us
  local copies, waits for them, and re-layouts: 7.6 us -> 2.41 us
  Pallas kernels: 20.1 us -> 22.9 us
  other arithmetic: 2.43 us -> 0.08 us
    all_to_all x0 -> x2, blocking collectives: none -> 43.6 us  [the longest x1 24.7 us: body(): lax.all_to_all(values, 'gz', split_axis=0, concat_axis=0, tiled=True)]
    all_to_all x2 -> x0, starting transfers between devices: 25.4 us -> none  [the longest x1 18.1 us: body(): lax.all_to_all(values, 'gz', split_axis=0, concat_axis=0, tiled=True)]
    all_to_all x2 -> x0, waiting for transfers between devices: 15.3 us -> none  [the longest x1 15.3 us: body(): lax.all_to_all(values, 'gz', split_axis=0, concat_axis=0, tiled=True)]
    ppermute x5 -> x4, waiting for transfers between devices: 7.12 us -> 0.01 us  [body(): lax.ppermute(s, AXES, mirror_pairs(*place))]
    ppermute x5 -> x4, starting transfers between devices: 19.9 us -> 15.5 us  [body(): lax.ppermute(s, AXES, mirror_pairs(*place))]
    unnamed x26 -> x16, local copies, waits for them, and re-layouts: 6.58 us -> 2.41 us
    ppermute x15, waiting for transfers between devices: 6.47 us -> 9.12 us  [receive(): return lax.ppermute(values, AXES, column_pairs(shift, flip))]
    mul x1 -> x0, other arithmetic: 2.33 us -> none  [body(): ta = jnp.asarray(first_forward()) * sign.astype(BF)[None, :, None]]
  transfers between devices with their start and end apart: 23 -> 20, of which waited for: 10 -> 8; matrix products, arithmetic and copies ran while one was open for 2% -> 0% of each run, Pallas kernels for 2% -> 7%
where the time goes in v1:
time: 134 us; the launch traced here: 133 us
  blocking collectives  63.4 us (47%)
  starting transfers between devices  31.5 us (24%)
  Pallas kernels  22.9 us (17%)
  waiting for transfers between devices  12.5 us (9%)
  local copies, waits for them, and re-layouts  2.41 us (2%)
    all_to_all x1, blocking collectives, body(): lax.all_to_all(values, 'gz', split_axis=0, concat_axis=0, tiled=True)  24.7 us
    all_to_all x1, blocking collectives, body(): lax.all_to_all(values, 'ta', split_axis=0, concat_axis=0, tiled=True)  19.8 us
    all_to_all x1, blocking collectives, spread(): return lax.all_to_all(values, 'ta', split_axis=0, concat_axis=0, tiled=True)  18.9 us
    ppermute x4, starting transfers between devices, body(): lax.ppermute(s, AXES, mirror_pairs(*place))  15.5 us
    ppermute x15, starting transfers between devices, receive(): return lax.ppermute(values, AXES, column_pairs(shift, flip))  14.5 us
    ppermute x15, waiting for transfers between devices, receive(): return lax.ppermute(values, AXES, column_pairs(shift, flip))  9.12 us
    pallas_call x1, Pallas kernels, spread(): call(forward_kernel, shape((16, 6, 16, 256), BF), [pltpu.VMEM((6, 8, 48,...  8.66 us
    pallas_call x1, Pallas kernels, body(): call(time_kernel, shape((16, 6, 16, 256), BF), [pltpu.VMEM((6, 12, 4864),...  7.46 us
  transfers between devices with their start and end apart: 20, of which 8 were waited for; matrix products, arithmetic and copies ran while one was open for 0% of the time, Pallas kernels for 7%

profile of v1, /device:TPU:32, one launch (start us, length us, event | category | flops | bytes accessed | tf_op | source)
XLA Modules:
  0.0 133.0 jit_solution(4080479169639906322)
XLA Ops:
  0.0 0.9 copy-done.3
  1.0 5.5 %collective-permute-start.5 = (bf16[48,1152]{1,0:T(8,128)(2,1)S(1)}, bf16[48,1152]{1,0:T(8,128)(2,1)S(1)}, u32[]{:S(2)}, u32[]{:S(2)}) collective-permute-start(bf16[48,1152]{1,0:T(8,128)(2,1)S(1)} %shard_map.130.refs_0_), channel_id=1, source_target_pairs={{4,0},{6,2},{5,1},{7,3},{8,4},{10,6},{9,5},{11,7},{12,8},{14,10},{... | collective-permute-start | bytes 331784 | tf_op jit(solution)/shard_map/ppermute | solution.py:500
  6.5 1.0 collective-permute-start.1
  7.5 1.0 collective-permute-start.3
  8.5 1.5 %collective-permute-done.5.refs_6_ = bf16[48,1152]{1,0:T(8,128)(2,1)S(1)} collective-permute-done((bf16[48,1152]{1,0:T(8,128)(2,1)S(1)}, bf16[48,1152]{1,0:T(8,128)(2,1)S(1)}, u32[]{:S(2)}, u32[]{:S(2)}) %collective-permute-start.5) | collective-permute-done | bytes 110624 | tf_op jit(solution)/shard_map/ppermute | solution.py:500
  10.0 2.9 %collective-permute-start.9 = (bf16[48,1152]{1,0:T(8,128)(2,1)S(1)}, bf16[48,1152]{1,0:T(8,128)(2,1)S(1)}, u32[]{:S(2)}, u32[]{:S(2)}) collective-permute-start(bf16[48,1152]{1,0:T(8,128)(2,1)S(1)} %collective-permute-done.5.refs_6_), channel_id=1, source_target_pairs={{1,0},{3,2},{4,1},{6,3},{5,4},{7,6},{8,5},{10,7},{9,8},{11,10},{12... | collective-permute-start | bytes 331784 | tf_op jit(solution)/shard_map/ppermute | solution.py:500
  12.9 3.0 %collective-permute-done.7.refs_8_ = bf16[48,1152]{1,0:T(8,128)(2,1)S(1)} collective-permute-done((bf16[48,1152]{1,0:T(8,128)(2,1)S(1)}, bf16[48,1152]{1,0:T(8,128)(2,1)S(1)}, u32[]{:S(2)}, u32[]{:S(2)}) %collective-permute-start.7) | collective-permute-done | bytes 110624 | tf_op jit(solution)/shard_map/ppermute | solution.py:500
  15.9 1.6 %collective-permute-start.13 = (bf16[48,1152]{1,0:T(8,128)(2,1)S(1)}, bf16[48,1152]{1,0:T(8,128)(2,1)S(1)}, u32[]{:S(2)}, u32[]{:S(2)}) collective-permute-start(bf16[48,1152]{1,0:T(8,128)(2,1)S(1)} %collective-permute-done.5.refs_6_), channel_id=1, source_target_pairs={{4,0},{6,2},{5,1},{7,3},{8,4},{10,6},{9,5},{11,7},{12,8},{14,10},{... | collective-permute-start | bytes 331784 | tf_op jit(solution)/shard_map/ppermute | solution.py:500
  17.5 0.9 collective-permute-start.11
  19.1 3.6 %collective-permute-done.13.refs_14_ = bf16[48,1152]{1,0:T(8,128)(2,1)S(1)} collective-permute-done((bf16[48,1152]{1,0:T(8,128)(2,1)S(1)}, bf16[48,1152]{1,0:T(8,128)(2,1)S(1)}, u32[]{:S(2)}, u32[]{:S(2)}) %collective-permute-start.13) | collective-permute-done | bytes 110624 | tf_op jit(solution)/shard_map/ppermute | solution.py:500
  24.7 2.5 %shard_map.131 = (bf16[5,48,1152]{2,1,0:T(8,128)(2,1)}, bf16[48,1152]{1,0:T(8,128)(2,1)}, bf16[24,1152]{1,0:T(8,128)(2,1)}, bf16[8,1152]{1,0:T(8,128)(2,1)}) custom-call(f32[6,12,9216]{2,1,0:T(8,128)} %refs_0_.1, bf16[48,1152]{1,0:T(8,128)(2,1)S(1)} %shard_map.130.refs_0_, bf16[48,1152]{1,0:T(8,128)(2,1)S(1)} %collective-permute-done.refs_1_, ...), custom_call_target="tpu_custom_call" | custom-call | flops 100000000 | bytes 4000000 | tf_op jit(solution)/shard_map/pallas_call | solution.py:530
  27.2 7.4 %collective-permute-start.15 = (bf16[5,48,1152]{2,1,0:T(8,128)(2,1)}, bf16[5,48,1152]{2,1,0:T(8,128)(2,1)S(1)}, u32[]{:S(2)}, u32[]{:S(2)}) collective-permute-start(bf16[5,48,1152]{2,1,0:T(8,128)(2,1)} %get-tuple-element.77), channel_id=1, source_target_pairs={{255,0},{254,1},{253,2},{252,3},{251,4},{250,5},{249,6},{248,7},{2... | collective-permute-start | bytes 1658888 | tf_op jit(solution)/shard_map/ppermute | solution.py:540
  34.6 2.2 %collective-permute-start.16 = (bf16[48,1152]{1,0:T(8,128)(2,1)}, bf16[48,1152]{1,0:T(8,128)(2,1)S(1)}, u32[]{:S(2)}, u32[]{:S(2)}) collective-permute-start(bf16[48,1152]{1,0:T(8,128)(2,1)} %get-tuple-element.78), channel_id=1, source_target_pairs={{15,0},{14,1},{13,2},{12,3},{11,4},{10,5},{9,6},{8,7},{7,8},{6,9},... | collective-permute-start | bytes 331784 | tf_op jit(solution)/shard_map/ppermute | solution.py:540
  36.8 3.7 %collective-permute-start.17 = (bf16[24,1152]{1,0:T(8,128)(2,1)}, bf16[24,1152]{1,0:T(8,128)(2,1)S(1)}, u32[]{:S(2)}, u32[]{:S(2)}) collective-permute-start(bf16[24,1152]{1,0:T(8,128)(2,1)} %get-tuple-element.79), channel_id=1, source_target_pairs={{241,0},{240,1},{255,2},{254,3},{253,4},{252,5},{251,6},{250,7},{2... | collective-permute-start | bytes 165896 | tf_op jit(solution)/shard_map/ppermute | solution.py:540
  40.4 2.2 %collective-permute-start.18 = (bf16[8,1152]{1,0:T(8,128)(2,1)}, bf16[8,1152]{1,0:T(8,128)(2,1)S(1)}, u32[]{:S(2)}, u32[]{:S(2)}) collective-permute-start(bf16[8,1152]{1,0:T(8,128)(2,1)} %get-tuple-element.80), channel_id=1, source_target_pairs={{1,0},{0,1},{15,2},{14,3},{13,4},{12,5},{11,6},{10,7},{9,8},{8,9},... | collective-permute-start | bytes 55304 | tf_op jit(solution)/shard_map/ppermute | solution.py:540
  42.7 27.5 %conditional.1 = (bf16[16,6,16,256]{3,2,1,0:T(8,128)(2,1)S(1)}) conditional(s32[]{:T(128)} %convert_element_type.3, () %tuple.11, (s32[4]{0:T(128)S(1)}, f32[1,384]{1,0:T(1,128)S(1)}, bf16[48,1152]{1,0:T(8,128)(2,1)S(1)}, bf16[48,1152]{1,0:T(8,128)(2,1)S(1)}, bf16[48,1152]{1,0:T(8,128)(2,1)S(1)}, /*index=5*/bf16[48,1152]{1,0:T(8,128)(2,1)S(1)}, ...), branch_computations={%region_0.1_spmd, %region_1.2_spmd} | conditional | flops 100000000 | bytes 5572872 | solution.py:560
  42.7 8.7 %branch_1_fun.1 = bf16[16,6,16,256]{3,2,1,0:T(8,128)(2,1)} custom-call(s32[4]{0:T(128)S(1)} %get-tuple-element.50.info_ref, f32[1,384]{1,0:T(1,128)S(1)} %get-tuple-element.51.sign_ref, bf16[48,1152]{1,0:T(8,128)(2,1)S(1)} %get-tuple-element.52.refs_0_, bf16[48,1152]{1,0:T(8,128)(2,1)S(1)} %get-tuple-element.53.refs_1_, ...), custom_call_target="tpu_custom_call" | custom-call | flops 100000000 | bytes 4000000 | tf_op jit(solution)/shard_map/cond/branch_1_fun/pallas_call | solution.py:542
  51.4 18.9 %all_to_all.14 = bf16[16,6,16,256]{3,2,1,0:T(8,128)(2,1)S(1)} all-to-all(bf16[16,6,16,256]{3,2,1,0:T(8,128)(2,1)} %branch_1_fun.1), channel_id=1, replica_groups=mesh['ta'=16,'gz'=8,'gy'=2] {'ta'}, dimensions={0} | all-to-all | bytes 1572864 | tf_op jit(solution)/shard_map/cond/branch_1_fun/all_to_all | solution.py:558
  71.8 7.5 %shard_map.132 = bf16[16,6,16,256]{3,2,1,0:T(8,128)(2,1)} custom-call(f32[6,12,9216]{2,1,0:T(8,128)} %refs_0_.1, bf16[5,48,1152]{2,1,0:T(8,128)(2,1)} %copy-done.4, bf16[48,1152]{1,0:T(8,128)(2,1)} %copy-done.5, bf16[24,1152]{1,0:T(8,128)(2,1)} %copy-done.6, bf16[8,1152]{1,0:T(8,128)(2,1)} %copy-done.7, bf16[192,192]{1,0:T(8,128)(2,1)} %constant.76.clone.refs_5_, ...), custom_call_target="tpu_custom_call" | custom-call | flops 100000000 | bytes 4000000 | tf_op jit(solution)/shard_map/pallas_call | solution.py:571
  79.3 19.8 %all_to_all.15.in_ref = bf16[16,6,16,256]{3,2,1,0:T(8,128)(2,1)S(1)} all-to-all(bf16[16,6,16,256]{3,2,1,0:T(8,128)(2,1)} %shard_map.132), channel_id=1, replica_groups=mesh['ta'=16,'gz'=8,'gy'=2] {'ta'}, dimensions={0} | all-to-all | bytes 1572864 | tf_op jit(solution)/shard_map/all_to_all | solution.py:586
  100.0 24.7 %all_to_all.16.in_ref = bf16[8,6,16,256]{3,2,1,0:T(8,128)(2,1)S(1)} all-to-all(bf16[8,6,16,256]{3,2,1,0:T(8,128)(2,1)S(1)} %shard_map.133), channel_id=1, replica_groups=mesh['ta'=16,'gz'=8,'gy'=2] {'gz'}, dimensions={0} | all-to-all | bytes 786432 | tf_op jit(solution)/shard_map/all_to_all | solution.py:590
  124.7 2.7 %shard_map.134 = (f32[6,6,1152]{2,1,0:T(8,128)S(1)}, bf16[48,1152]{1,0:T(8,128)(2,1)S(1)}) custom-call(s32[4]{0:T(128)S(1)} %pad_add_fusion.info_ref, bf16[8,6,16,256]{3,2,1,0:T(8,128)(2,1)S(1)} %all_to_all.16.in_ref, bf16[1,1024,768]{2,1,0:T(8,128)(2,1)S(1)} %copy-done, bf16[2,640,384]{2,1,0:T(8,128)(2,1)S(1)} %copy-done.1, ...), custom_call_target="tpu_custom_call" | custom-call | flops 100000000 | bytes 4000000 | tf_op jit(solution)/shard_map/pallas_call | solution.py:591
  127.4 1.4 %collective-permute-start.19 = (bf16[48,1152]{1,0:T(8,128)(2,1)S(1)}, bf16[48,1152]{1,0:T(8,128)(2,1)S(1)}, u32[]{:S(2)}, u32[]{:S(2)}) collective-permute-start(bf16[48,1152]{1,0:T(8,128)(2,1)S(1)} %get-tuple-element.82), channel_id=1, source_target_pairs={{0,1},{1,0},{2,3},{3,2},{4,5},{5,4},{6,7},{7,6},{8,9},{9,8},{10,11... | collective-permute-start | bytes 331784 | tf_op jit(solution)/shard_map/ppermute | solution.py:604
  128.9 3.4 %collective-permute-done.19.other_ref = bf16[48,1152]{1,0:T(8,128)(2,1)S(1)} collective-permute-done((bf16[48,1152]{1,0:T(8,128)(2,1)S(1)}, bf16[48,1152]{1,0:T(8,128)(2,1)S(1)}, u32[]{:S(2)}, u32[]{:S(2)}) %collective-permute-start.19) | collective-permute-done | bytes 110624 | tf_op jit(solution)/shard_map/ppermute | solution.py:604
  (45 shorter events, 5.7 us)
Async XLA Ops:
  0.0 0.9 copy-start.3
  1.0 9.0 %collective-permute-start.5 = (bf16[48,1152]{1,0:T(8,128)(2,1)S(1)}, bf16[48,1152]{1,0:T(8,128)(2,1)S(1)}, u32[]{:S(2)}, u32[]{:S(2)}) collective-permute-start(bf16[48,1152]{1,0:T(8,128)(2,1)S(1)} %shard_map.130.refs_0_), channel_id=1, source_target_pairs={{4,0},{6,2},{5,1},{7,3},{8,4},{10,6},{9,5},{11,7},{12,8},{14,10},{... | collective-permute-start | bytes 331784 | tf_op jit(solution)/shard_map/ppermute | solution.py:500
  6.5 9.5 %collective-permute-start.7 = (bf16[48,1152]{1,0:T(8,128)(2,1)S(1)}, bf16[48,1152]{1,0:T(8,128)(2,1)S(1)}, u32[]{:S(2)}, u32[]{:S(2)}) collective-permute-start(bf16[48,1152]{1,0:T(8,128)(2,1)S(1)} %shard_map.130.refs_0_), channel_id=1, source_target_pairs={{12,0},{14,2},{13,1},{15,3},{0,4},{2,6},{1,5},{3,7},{4,8},{6,10},{... | collective-permute-start | bytes 331784 | tf_op jit(solution)/shard_map/ppermute | solution.py:500
  6.5 11.1 %collective-permute-start.1 = (bf16[48,1152]{1,0:T(8,128)(2,1)S(1)}, bf16[48,1152]{1,0:T(8,128)(2,1)S(1)}, u32[]{:S(2)}, u32[]{:S(2)}) collective-permute-start(bf16[48,1152]{1,0:T(8,128)(2,1)S(1)} %shard_map.130.refs_0_), channel_id=1, source_target_pairs={{1,0},{3,2},{4,1},{6,3},{5,4},{7,6},{8,5},{10,7},{9,8},{11,10},{12... | collective-permute-start | bytes 331784 | tf_op jit(solution)/shard_map/ppermute | solution.py:500
  7.5 11.0 %collective-permute-start.3 = (bf16[48,1152]{1,0:T(8,128)(2,1)S(1)}, bf16[48,1152]{1,0:T(8,128)(2,1)S(1)}, u32[]{:S(2)}, u32[]{:S(2)}) collective-permute-start(bf16[48,1152]{1,0:T(8,128)(2,1)S(1)} %shard_map.130.refs_0_), channel_id=1, source_target_pairs={{13,0},{15,2},{0,1},{2,3},{1,4},{3,6},{4,5},{6,7},{5,8},{7,10},{8,... | collective-permute-start | bytes 331784 | tf_op jit(solution)/shard_map/ppermute | solution.py:500
  8.5 10.0 %collective-permute-start = (bf16[48,1152]{1,0:T(8,128)(2,1)S(1)}, bf16[48,1152]{1,0:T(8,128)(2,1)S(1)}, u32[]{:S(2)}, u32[]{:S(2)}) collective-permute-start(bf16[48,1152]{1,0:T(8,128)(2,1)S(1)} %shard_map.130.refs_0_), channel_id=1, source_target_pairs={{2,0},{0,2},{3,1},{1,3},{6,4},{4,6},{7,5},{5,7},{10,8},{8,10},{11,... | collective-permute-start | bytes 331784 | tf_op jit(solution)/shard_map/ppermute | solution.py:500
  10.0 9.0 %collective-permute-start.9 = (bf16[48,1152]{1,0:T(8,128)(2,1)S(1)}, bf16[48,1152]{1,0:T(8,128)(2,1)S(1)}, u32[]{:S(2)}, u32[]{:S(2)}) collective-permute-start(bf16[48,1152]{1,0:T(8,128)(2,1)S(1)} %collective-permute-done.5.refs_6_), channel_id=1, source_target_pairs={{1,0},{3,2},{4,1},{6,3},{5,4},{7,6},{8,5},{10,7},{9,8},{11,10},{12... | collective-permute-start | bytes 331784 | tf_op jit(solution)/shard_map/ppermute | solution.py:500
  15.9 6.7 %collective-permute-start.13 = (bf16[48,1152]{1,0:T(8,128)(2,1)S(1)}, bf16[48,1152]{1,0:T(8,128)(2,1)S(1)}, u32[]{:S(2)}, u32[]{:S(2)}) collective-permute-start(bf16[48,1152]{1,0:T(8,128)(2,1)S(1)} %collective-permute-done.5.refs_6_), channel_id=1, source_target_pairs={{4,0},{6,2},{5,1},{7,3},{8,4},{10,6},{9,5},{11,7},{12,8},{14,10},{... | collective-permute-start | bytes 331784 | tf_op jit(solution)/shard_map/ppermute | solution.py:500
  17.5 5.2 %collective-permute-start.11 = (bf16[48,1152]{1,0:T(8,128)(2,1)S(1)}, bf16[48,1152]{1,0:T(8,128)(2,1)S(1)}, u32[]{:S(2)}, u32[]{:S(2)}) collective-permute-start(bf16[48,1152]{1,0:T(8,128)(2,1)S(1)} %collective-permute-done.7.refs_8_), channel_id=1, source_target_pairs={{13,0},{15,2},{0,1},{2,3},{1,4},{3,6},{4,5},{6,7},{5,8},{7,10},{8,... | collective-permute-start | bytes 331784 | tf_op jit(solution)/shard_map/ppermute | solution.py:500
  18.5 4.7 %collective-permute-start.6 = (bf16[48,1152]{1,0:T(8,128)(2,1)S(1)}, bf16[48,1152]{1,0:T(8,128)(2,1)S(1)}, u32[]{:S(2)}, u32[]{:S(2)}) collective-permute-start(bf16[48,1152]{1,0:T(8,128)(2,1)S(1)} %collective-permute-done.5.refs_6_), channel_id=1, source_target_pairs={{2,0},{0,2},{3,1},{1,3},{6,4},{4,6},{7,5},{5,7},{10,8},{8,10},{11,... | collective-permute-start | bytes 331784 | tf_op jit(solution)/shard_map/ppermute | solution.py:500
  18.5 4.8 %collective-permute-start.8 = (bf16[48,1152]{1,0:T(8,128)(2,1)S(1)}, bf16[48,1152]{1,0:T(8,128)(2,1)S(1)}, u32[]{:S(2)}, u32[]{:S(2)}) collective-permute-start(bf16[48,1152]{1,0:T(8,128)(2,1)S(1)} %collective-permute-done.7.refs_8_), channel_id=1, source_target_pairs={{2,0},{0,2},{3,1},{1,3},{6,4},{4,6},{7,5},{5,7},{10,8},{8,10},{11,... | collective-permute-start | bytes 331784 | tf_op jit(solution)/shard_map/ppermute | solution.py:500
  19.0 4.7 %collective-permute-start.2 = (bf16[48,1152]{1,0:T(8,128)(2,1)S(1)}, bf16[48,1152]{1,0:T(8,128)(2,1)S(1)}, u32[]{:S(2)}, u32[]{:S(2)}) collective-permute-start(bf16[48,1152]{1,0:T(8,128)(2,1)S(1)} %collective-permute-done.1.refs_2_), channel_id=1, source_target_pairs={{2,0},{0,2},{3,1},{1,3},{6,4},{4,6},{7,5},{5,7},{10,8},{8,10},{11,... | collective-permute-start | bytes 331784 | tf_op jit(solution)/shard_map/ppermute | solution.py:500
  22.7 1.3 collective-permute-start.4
  22.7 1.5 %collective-permute-start.10 = (bf16[48,1152]{1,0:T(8,128)(2,1)S(1)}, bf16[48,1152]{1,0:T(8,128)(2,1)S(1)}, u32[]{:S(2)}, u32[]{:S(2)}) collective-permute-start(bf16[48,1152]{1,0:T(8,128)(2,1)S(1)} %collective-permute-done.9.refs_10_), channel_id=1, source_target_pairs={{2,0},{0,2},{3,1},{1,3},{6,4},{4,6},{7,5},{5,7},{10,8},{8,10},{11,... | collective-permute-start | bytes 331784 | tf_op jit(solution)/shard_map/ppermute | solution.py:500
  23.2 1.3 collective-permute-start.14
  23.3 1.4 %collective-permute-start.12 = (bf16[48,1152]{1,0:T(8,128)(2,1)S(1)}, bf16[48,1152]{1,0:T(8,128)(2,1)S(1)}, u32[]{:S(2)}, u32[]{:S(2)}) collective-permute-start(bf16[48,1152]{1,0:T(8,128)(2,1)S(1)} %collective-permute-done.11.refs_12_), channel_id=1, source_target_pairs={{2,0},{0,2},{3,1},{1,3},{6,4},{4,6},{7,5},{5,7},{10,8},{8,10},{11,... | collective-permute-start | bytes 331784 | tf_op jit(solution)/shard_map/ppermute | solution.py:500
  27.2 43.2 %collective-permute-start.15 = (bf16[5,48,1152]{2,1,0:T(8,128)(2,1)}, bf16[5,48,1152]{2,1,0:T(8,128)(2,1)S(1)}, u32[]{:S(2)}, u32[]{:S(2)}) collective-permute-start(bf16[5,48,1152]{2,1,0:T(8,128)(2,1)} %get-tuple-element.77), channel_id=1, source_target_pairs={{255,0},{254,1},{253,2},{252,3},{251,4},{250,5},{249,6},{248,7},{2... | collective-permute-start | bytes 1658888 | tf_op jit(solution)/shard_map/ppermute | solution.py:540
  34.6 35.8 %collective-permute-start.16 = (bf16[48,1152]{1,0:T(8,128)(2,1)}, bf16[48,1152]{1,0:T(8,128)(2,1)S(1)}, u32[]{:S(2)}, u32[]{:S(2)}) collective-permute-start(bf16[48,1152]{1,0:T(8,128)(2,1)} %get-tuple-element.78), channel_id=1, source_target_pairs={{15,0},{14,1},{13,2},{12,3},{11,4},{10,5},{9,6},{8,7},{7,8},{6,9},... | collective-permute-start | bytes 331784 | tf_op jit(solution)/shard_map/ppermute | solution.py:540
  36.8 33.5 %collective-permute-start.17 = (bf16[24,1152]{1,0:T(8,128)(2,1)}, bf16[24,1152]{1,0:T(8,128)(2,1)S(1)}, u32[]{:S(2)}, u32[]{:S(2)}) collective-permute-start(bf16[24,1152]{1,0:T(8,128)(2,1)} %get-tuple-element.79), channel_id=1, source_target_pairs={{241,0},{240,1},{255,2},{254,3},{253,4},{252,5},{251,6},{250,7},{2... | collective-permute-start | bytes 165896 | tf_op jit(solution)/shard_map/ppermute | solution.py:540
  40.4 29.9 %collective-permute-start.18 = (bf16[8,1152]{1,0:T(8,128)(2,1)}, bf16[8,1152]{1,0:T(8,128)(2,1)S(1)}, u32[]{:S(2)}, u32[]{:S(2)}) collective-permute-start(bf16[8,1152]{1,0:T(8,128)(2,1)} %get-tuple-element.80), channel_id=1, source_target_pairs={{1,0},{0,1},{15,2},{14,3},{13,4},{12,5},{11,6},{10,7},{9,8},{8,9},... | collective-permute-start | bytes 55304 | tf_op jit(solution)/shard_map/ppermute | solution.py:540
  70.3 28.8 %copy-start.2 = (bf16[2,4,128,192]{3,2,1,0:T(8,128)(2,1)S(1)}, bf16[2,4,128,192]{3,2,1,0:T(8,128)(2,1)}, u32[]{:S(2)}) copy-start(bf16[2,4,128,192]{3,2,1,0:T(8,128)(2,1)} %constant.81.clone.table_ref) | copy-start | bytes 1179652
  79.3 45.4 %copy-start = (bf16[1,1024,768]{2,1,0:T(8,128)(2,1)S(1)}, bf16[1,1024,768]{2,1,0:T(8,128)(2,1)}, u32[]{:S(2)}) copy-start(bf16[1,1024,768]{2,1,0:T(8,128)(2,1)} %constant.82.clone.tb_source) | copy-start | bytes 4718596
  79.3 45.4 %copy-start.1 = (bf16[2,640,384]{2,1,0:T(8,128)(2,1)S(1)}, bf16[2,640,384]{2,1,0:T(8,128)(2,1)}, u32[]{:S(2)}) copy-start(bf16[2,640,384]{2,1,0:T(8,128)(2,1)} %constant.83.clone.ta_source) | copy-start | bytes 2949124
  127.4 4.8 %collective-permute-start.19 = (bf16[48,1152]{1,0:T(8,128)(2,1)S(1)}, bf16[48,1152]{1,0:T(8,128)(2,1)S(1)}, u32[]{:S(2)}, u32[]{:S(2)}) collective-permute-start(bf16[48,1152]{1,0:T(8,128)(2,1)S(1)} %get-tuple-element.82), channel_id=1, source_target_pairs={{0,1},{1,0},{2,3},{3,2},{4,5},{5,4},{6,7},{7,6},{8,9},{9,8},{10,11... | collective-permute-start | bytes 331784 | tf_op jit(solution)/shard_map/ppermute | solution.py:604
  (4 other events, 2.7 us)

commit v2 on v1

--- a/solution.py
+++ b/solution.py
@@ -215,25 +215,36 @@
         plane -= count
 
 
-def weight_send_kernel(source_ref, *refs):
-    refs = refs[16:]
-    plane_ref, line_ref, corner_ref, work, rows, kernel_ref, arrival = refs[len(PARTS) :]
-    copy = pltpu.make_async_copy(source_ref.at[:, :, pl.ds(4608, 4608)], kernel_ref, arrival)
+def weight_line_kernel(source_ref, line_ref, corner_ref, rows, kernel_ref, arrival):
+    copy = pltpu.make_async_copy(
+        source_ref.at[:, 0:8, pl.ds(4608, 4608)], kernel_ref, arrival
+    )
     copy.start()
     copy.wait()
     rows[...] = jnp.zeros_like(rows)
     for w in range(6):
         for c in range(4):
+            piece = kernel_ref[w, 0:1, 1152 * c : 1152 * (c + 1)]
+            rows[4 * w + c : 4 * w + c + 1, :] = piece
+    line_ref[...] = rows[4:28, :].astype(BF)
+    corner_ref[...] = rows[0:8, :].astype(BF)
+
+
+def weight_send_kernel(source_ref, *refs):
+    refs = refs[18:]
+    plane_ref, work, kernel_ref, arrival = refs[len(PARTS) :]
+    copy = pltpu.make_async_copy(source_ref.at[:, :, pl.ds(4608, 4608)], kernel_ref, arrival)
+    copy.start()
+    copy.wait()
+    for w in range(6):
+        for c in range(4):
             piece = kernel_ref[w, :, 1152 * c : 1152 * (c + 1)]
             work[12 * c : 12 * c + 12, :] = piece
-            rows[4 * w + c : 4 * w + c + 1, :] = piece[0:1]
         if w == 0:
             plane_ref[...] = work[...].astype(BF)
         else:
             part, place = part_of(w - 1)
             refs[part][place] = work[...].astype(BF)
-    line_ref[...] = rows[4:28, :].astype(BF)
-    corner_ref[...] = rows[0:8, :].astype(BF)
 
 
 def own_weights(kernel_ref, eye_ref, weight, work):
@@ -527,17 +538,34 @@
     block = call(raw_kernel, shape((48, 1152), BF), [pltpu.VMEM((48, 1152), F32)], vmem=8)(current)
     blocks = gather_column(block)
 
+    line, corner = call(
+        weight_line_kernel,
+        [shape((24, 1152), BF), shape((8, 1152), BF)],
+        [
+            pltpu.VMEM((32, 1152), F32),
+            pltpu.VMEM((6, 8, 4608), F32),
+            pltpu.SemaphoreType.DMA,
+        ],
+        in_specs=[anywhere],
+        vmem=59,
+    )(kernel)
+    line = lax.ppermute(line, AXES, mirror_pairs(15, 8))
+    corner = lax.ppermute(corner, AXES, mirror_pairs(16, 8))
     sent = call(
         weight_send_kernel,
-        [shape((n, 48, 1152), BF) for n in PARTS]
-        + [shape((48, 1152), BF), shape((24, 1152), BF), shape((8, 1152), BF)],
-        [pltpu.VMEM((48, 1152), F32), pltpu.VMEM((32, 1152), F32)]
-        + [pltpu.VMEM((6, 12, 4608), F32), pltpu.SemaphoreType.DMA],
-        in_specs=[anywhere] * 17,
+        [shape((n, 48, 1152), BF) for n in PARTS] + [shape((48, 1152), BF)],
+        [
+            pltpu.VMEM((48, 1152), F32),
+            pltpu.VMEM((6, 12, 4608), F32),
+            pltpu.SemaphoreType.DMA,
+        ],
+        in_specs=[anywhere] * 19,
         vmem=59,
-    )(kernel, *blocks)
-    places = ((15, 7),) * len(PARTS) + ((16, 7), (15, 8), (16, 8))
+    )(kernel, *blocks, line, corner)
+    places = ((15, 7),) * len(PARTS) + ((16, 7),)
     arrived = [lax.ppermute(s, AXES, mirror_pairs(*place)) for s, place in zip(sent, places)]
+    arrived += [line, corner]
+
     def spread(*operands):
         values = call(
             forward_kernel,

time: 134 us -> 139 us (1.037)
  starting transfers between devices: 31.5 us -> 34.2 us
  blocking collectives: 63.4 us -> 66 us
  Pallas kernels: 22.9 us -> 24.8 us
    ppermute x0 -> x2, starting transfers between devices: none -> 6.76 us  [the longest x1 4.84 us: body(): line = lax.ppermute(line, AXES, mirror_pairs(15, 8))]
    ppermute x4 -> x2, starting transfers between devices: 15.5 us -> 9.13 us  [body(): lax.ppermute(s, AXES, mirror_pairs(*place))]
    all_to_all x1, blocking collectives: 24.7 us -> 29 us  [body(): lax.all_to_all(values, 'gz', split_axis=0, concat_axis=0, tiled=True)]
    ppermute x15, starting transfers between devices: 14.5 us -> 17.6 us  [receive(): return lax.ppermute(values, AXES, column_pairs(shift, flip))]
    all_to_all x1, blocking collectives: 19.8 us -> 17.7 us  [body(): lax.all_to_all(values, 'ta', split_axis=0, concat_axis=0, tiled=True)]
    pallas_call x0 -> x1, Pallas kernels: none -> 1.9 us  [body(): call(weight_line_kernel, [shape((24, 1152), BF), shape((8, 1152), BF)], [...]
  transfers between devices with their start and end apart: 20 -> 20, of which waited for: 8 -> 8; matrix products, arithmetic and copies ran while one was open for 0% -> 0% of each run, Pallas kernels for 7% -> 6%
where the time goes in v2:
time: 139 us
  blocking collectives  66 us (47%)
  starting transfers between devices  34.2 us (25%)
  Pallas kernels  24.8 us (18%)
  waiting for transfers between devices  12.2 us (9%)
  local copies, waits for them, and re-layouts  1.48 us (1%)
    all_to_all x1, blocking collectives, body(): lax.all_to_all(values, 'gz', split_axis=0, concat_axis=0, tiled=True)  29 us
    all_to_all x1, blocking collectives, spread(): return lax.all_to_all(values, 'ta', split_axis=0, concat_axis=0, tiled=True)  19.3 us
    all_to_all x1, blocking collectives, body(): lax.all_to_all(values, 'ta', split_axis=0, concat_axis=0, tiled=True)  17.7 us
    ppermute x15, starting transfers between devices, receive(): return lax.ppermute(values, AXES, column_pairs(shift, flip))  17.6 us
    ppermute x2, starting transfers between devices, body(): lax.ppermute(s, AXES, mirror_pairs(*place))  9.13 us
    pallas_call x1, Pallas kernels, spread(): call(forward_kernel, shape((16, 6, 16, 256), BF), [pltpu.VMEM((6, 8, 48,...  8.65 us
    ppermute x15, waiting for transfers between devices, receive(): return lax.ppermute(values, AXES, column_pairs(shift, flip))  8.16 us
    pallas_call x1, Pallas kernels, body(): call(time_kernel, shape((16, 6, 16, 256), BF), [pltpu.VMEM((6, 12, 4864),...  7.45 us
  transfers between devices with their start and end apart: 20, of which 8 were waited for; matrix products, arithmetic and copies ran while one was open for 0% of the time, Pallas kernels for 6%

profile of v2, /device:TPU:32, one launch (start us, length us, event | category | flops | bytes accessed | tf_op | source)
XLA Modules:
  0.0 138.9 jit_solution(13208075316299984804)
XLA Ops:
  0.0 1.9 %shard_map.131 = (bf16[24,1152]{1,0:T(8,128)(2,1)}, bf16[8,1152]{1,0:T(8,128)(2,1)}) custom-call(f32[6,12,9216]{2,1,0:T(8,128)} %refs_0_.1), custom_call_target="tpu_custom_call" | custom-call | flops 100000000 | bytes 4000000 | tf_op jit(solution)/shard_map/pallas_call | solution.py:541
  1.9 4.8 %collective-permute-start.15 = (bf16[24,1152]{1,0:T(8,128)(2,1)}, bf16[24,1152]{1,0:T(8,128)(2,1)S(1)}, u32[]{:S(2)}, u32[]{:S(2)}) collective-permute-start(bf16[24,1152]{1,0:T(8,128)(2,1)} %get-tuple-element.77), channel_id=1, source_target_pairs={{241,0},{240,1},{255,2},{254,3},{253,4},{252,5},{251,6},{250,7},{2... | collective-permute-start | bytes 165896 | tf_op jit(solution)/shard_map/ppermute | solution.py:552
  6.8 1.9 %collective-permute-start.16 = (bf16[8,1152]{1,0:T(8,128)(2,1)}, bf16[8,1152]{1,0:T(8,128)(2,1)S(1)}, u32[]{:S(2)}, u32[]{:S(2)}) collective-permute-start(bf16[8,1152]{1,0:T(8,128)(2,1)} %get-tuple-element.78), channel_id=1, source_target_pairs={{1,0},{0,1},{15,2},{14,3},{13,4},{12,5},{11,6},{10,7},{9,8},{8,9},... | collective-permute-start | bytes 55304 | tf_op jit(solution)/shard_map/ppermute | solution.py:553
  8.7 8.5 %collective-permute-start.5 = (bf16[48,1152]{1,0:T(8,128)(2,1)S(1)}, bf16[48,1152]{1,0:T(8,128)(2,1)S(1)}, u32[]{:S(2)}, u32[]{:S(2)}) collective-permute-start(bf16[48,1152]{1,0:T(8,128)(2,1)S(1)} %shard_map.130.refs_0_), channel_id=1, source_target_pairs={{4,0},{6,2},{5,1},{7,3},{8,4},{10,6},{9,5},{11,7},{12,8},{14,10},{... | collective-permute-start | bytes 331784 | tf_op jit(solution)/shard_map/ppermute | solution.py:511
  17.2 1.0 collective-permute-start.1
  18.2 2.4 %collective-permute-start.3 = (bf16[48,1152]{1,0:T(8,128)(2,1)S(1)}, bf16[48,1152]{1,0:T(8,128)(2,1)S(1)}, u32[]{:S(2)}, u32[]{:S(2)}) collective-permute-start(bf16[48,1152]{1,0:T(8,128)(2,1)S(1)} %shard_map.130.refs_0_), channel_id=1, source_target_pairs={{13,0},{15,2},{0,1},{2,3},{1,4},{3,6},{4,5},{6,7},{5,8},{7,10},{8,... | collective-permute-start | bytes 331784 | tf_op jit(solution)/shard_map/ppermute | solution.py:511
  21.0 1.9 %collective-permute-start.9 = (bf16[48,1152]{1,0:T(8,128)(2,1)S(1)}, bf16[48,1152]{1,0:T(8,128)(2,1)S(1)}, u32[]{:S(2)}, u32[]{:S(2)}) collective-permute-start(bf16[48,1152]{1,0:T(8,128)(2,1)S(1)} %collective-permute-done.5.refs_6_), channel_id=1, source_target_pairs={{1,0},{3,2},{4,1},{6,3},{5,4},{7,6},{8,5},{10,7},{9,8},{11,10},{12... | collective-permute-start | bytes 331784 | tf_op jit(solution)/shard_map/ppermute | solution.py:511
  22.9 3.5 %collective-permute-done.7.refs_8_ = bf16[48,1152]{1,0:T(8,128)(2,1)S(1)} collective-permute-done((bf16[48,1152]{1,0:T(8,128)(2,1)S(1)}, bf16[48,1152]{1,0:T(8,128)(2,1)S(1)}, u32[]{:S(2)}, u32[]{:S(2)}) %collective-permute-start.7) | collective-permute-done | bytes 110624 | tf_op jit(solution)/shard_map/ppermute | solution.py:511
  26.4 1.2 collective-permute-start.13
  27.6 1.0 collective-permute-start.11
  29.2 3.3 %collective-permute-done.13.refs_14_ = bf16[48,1152]{1,0:T(8,128)(2,1)S(1)} collective-permute-done((bf16[48,1152]{1,0:T(8,128)(2,1)S(1)}, bf16[48,1152]{1,0:T(8,128)(2,1)S(1)}, u32[]{:S(2)}, u32[]{:S(2)}) %collective-permute-start.13) | collective-permute-done | bytes 110624 | tf_op jit(solution)/shard_map/ppermute | solution.py:511
  34.5 2.5 %shard_map.132 = (bf16[5,48,1152]{2,1,0:T(8,128)(2,1)}, bf16[48,1152]{1,0:T(8,128)(2,1)}) custom-call(f32[6,12,9216]{2,1,0:T(8,128)} %refs_0_.1, bf16[48,1152]{1,0:T(8,128)(2,1)S(1)} %shard_map.130.refs_0_, bf16[48,1152]{1,0:T(8,128)(2,1)S(1)} %collective-permute-done.refs_1_, bf16[48,1152]{1,0:T(8,128)(2,1)S(1)} %collective-permute-done.1.refs_2_, ...), custom_call_target="tpu_custom_call" | custom-call | flops 100000000 | bytes 4000000 | tf_op jit(solution)/shard_map/pallas_call | solution.py:554
  36.9 8.4 %collective-permute-start.17 = (bf16[5,48,1152]{2,1,0:T(8,128)(2,1)}, bf16[5,48,1152]{2,1,0:T(8,128)(2,1)S(1)}, u32[]{:S(2)}, u32[]{:S(2)}) collective-permute-start(bf16[5,48,1152]{2,1,0:T(8,128)(2,1)} %get-tuple-element.79), channel_id=1, source_target_pairs={{255,0},{254,1},{253,2},{252,3},{251,4},{250,5},{249,6},{248,7},{2... | collective-permute-start | bytes 1658888 | tf_op jit(solution)/shard_map/ppermute | solution.py:566
  46.2 27.9 %conditional.1 = (bf16[16,6,16,256]{3,2,1,0:T(8,128)(2,1)S(1)}) conditional(s32[]{:T(128)} %convert_element_type.3, () %tuple.11, (s32[4]{0:T(128)S(1)}, f32[1,384]{1,0:T(1,128)S(1)}, bf16[48,1152]{1,0:T(8,128)(2,1)S(1)}, bf16[48,1152]{1,0:T(8,128)(2,1)S(1)}, bf16[48,1152]{1,0:T(8,128)(2,1)S(1)}, /*index=5*/bf16[48,1152]{1,0:T(8,128)(2,1)S(1)}, ...), branch_computations={%region_0.1_spmd, %region_1.2_spmd} | conditional | flops 100000000 | bytes 5572872 | solution.py:588
  46.2 8.7 %branch_1_fun.1 = bf16[16,6,16,256]{3,2,1,0:T(8,128)(2,1)} custom-call(s32[4]{0:T(128)S(1)} %get-tuple-element.50.info_ref, f32[1,384]{1,0:T(1,128)S(1)} %get-tuple-element.51.sign_ref, bf16[48,1152]{1,0:T(8,128)(2,1)S(1)} %get-tuple-element.52.refs_0_, bf16[48,1152]{1,0:T(8,128)(2,1)S(1)} %get-tuple-element.53.refs_1_, ...), custom_call_target="tpu_custom_call" | custom-call | flops 100000000 | bytes 4000000 | tf_op jit(solution)/shard_map/cond/branch_1_fun/pallas_call | solution.py:570
  54.8 19.3 %all_to_all.14 = bf16[16,6,16,256]{3,2,1,0:T(8,128)(2,1)S(1)} all-to-all(bf16[16,6,16,256]{3,2,1,0:T(8,128)(2,1)} %branch_1_fun.1), channel_id=1, replica_groups=mesh['ta'=16,'gz'=8,'gy'=2] {'ta'}, dimensions={0} | all-to-all | bytes 1572864 | tf_op jit(solution)/shard_map/cond/branch_1_fun/all_to_all | solution.py:586
  74.7 0.8 copy-done.4
  75.6 7.5 %shard_map.133 = bf16[16,6,16,256]{3,2,1,0:T(8,128)(2,1)} custom-call(f32[6,12,9216]{2,1,0:T(8,128)} %refs_0_.1, bf16[5,48,1152]{2,1,0:T(8,128)(2,1)} %copy-done.4, bf16[48,1152]{1,0:T(8,128)(2,1)} %copy-done.6, bf16[24,1152]{1,0:T(8,128)(2,1)} %copy-done.5, bf16[8,1152]{1,0:T(8,128)(2,1)} %copy-done.7, bf16[192,192]{1,0:T(8,128)(2,1)} %constant.76.clone.refs_5_, ...), custom_call_target="tpu_custom_call" | custom-call | flops 100000000 | bytes 4000000 | tf_op jit(solution)/shard_map/pallas_call | solution.py:599
  83.0 17.7 %all_to_all.15.in_ref = bf16[16,6,16,256]{3,2,1,0:T(8,128)(2,1)S(1)} all-to-all(bf16[16,6,16,256]{3,2,1,0:T(8,128)(2,1)} %shard_map.133), channel_id=1, replica_groups=mesh['ta'=16,'gz'=8,'gy'=2] {'ta'}, dimensions={0} | all-to-all | bytes 1572864 | tf_op jit(solution)/shard_map/all_to_all | solution.py:614
  100.8 0.8 shard_map.134
  101.6 29.0 %all_to_all.16.in_ref = bf16[8,6,16,256]{3,2,1,0:T(8,128)(2,1)S(1)} all-to-all(bf16[8,6,16,256]{3,2,1,0:T(8,128)(2,1)S(1)} %shard_map.134), channel_id=1, replica_groups=mesh['ta'=16,'gz'=8,'gy'=2] {'gz'}, dimensions={0} | all-to-all | bytes 786432 | tf_op jit(solution)/shard_map/all_to_all | solution.py:618
  130.6 2.7 %shard_map.135 = (f32[6,6,1152]{2,1,0:T(8,128)S(1)}, bf16[48,1152]{1,0:T(8,128)(2,1)S(1)}) custom-call(s32[4]{0:T(128)S(1)} %pad_add_fusion.info_ref, bf16[8,6,16,256]{3,2,1,0:T(8,128)(2,1)S(1)} %all_to_all.16.in_ref, bf16[1,1024,768]{2,1,0:T(8,128)(2,1)S(1)} %copy-done, bf16[2,640,384]{2,1,0:T(8,128)(2,1)S(1)} %copy-done.1, ...), custom_call_target="tpu_custom_call" | custom-call | flops 100000000 | bytes 4000000 | tf_op jit(solution)/shard_map/pallas_call | solution.py:619
  133.3 0.8 collective-permute-start.19
  134.1 4.1 %collective-permute-done.19.other_ref = bf16[48,1152]{1,0:T(8,128)(2,1)S(1)} collective-permute-done((bf16[48,1152]{1,0:T(8,128)(2,1)S(1)}, bf16[48,1152]{1,0:T(8,128)(2,1)S(1)}, u32[]{:S(2)}, u32[]{:S(2)}) %collective-permute-start.19) | collective-permute-done | bytes 110624 | tf_op jit(solution)/shard_map/ppermute | solution.py:632
  (46 shorter events, 5.3 us)
Async XLA Ops:
  1.9 18.7 %collective-permute-start.15 = (bf16[24,1152]{1,0:T(8,128)(2,1)}, bf16[24,1152]{1,0:T(8,128)(2,1)S(1)}, u32[]{:S(2)}, u32[]{:S(2)}) collective-permute-start(bf16[24,1152]{1,0:T(8,128)(2,1)} %get-tuple-element.77), channel_id=1, source_target_pairs={{241,0},{240,1},{255,2},{254,3},{253,4},{252,5},{251,6},{250,7},{2... | collective-permute-start | bytes 165896 | tf_op jit(solution)/shard_map/ppermute | solution.py:552
  6.8 11.5 %collective-permute-start.16 = (bf16[8,1152]{1,0:T(8,128)(2,1)}, bf16[8,1152]{1,0:T(8,128)(2,1)S(1)}, u32[]{:S(2)}, u32[]{:S(2)}) collective-permute-start(bf16[8,1152]{1,0:T(8,128)(2,1)} %get-tuple-element.78), channel_id=1, source_target_pairs={{1,0},{0,1},{15,2},{14,3},{13,4},{12,5},{11,6},{10,7},{9,8},{8,9},... | collective-permute-start | bytes 55304 | tf_op jit(solution)/shard_map/ppermute | solution.py:553
  8.7 12.3 %collective-permute-start.5 = (bf16[48,1152]{1,0:T(8,128)(2,1)S(1)}, bf16[48,1152]{1,0:T(8,128)(2,1)S(1)}, u32[]{:S(2)}, u32[]{:S(2)}) collective-permute-start(bf16[48,1152]{1,0:T(8,128)(2,1)S(1)} %shard_map.130.refs_0_), channel_id=1, source_target_pairs={{4,0},{6,2},{5,1},{7,3},{8,4},{10,6},{9,5},{11,7},{12,8},{14,10},{... | collective-permute-start | bytes 331784 | tf_op jit(solution)/shard_map/ppermute | solution.py:511
  17.2 9.2 %collective-permute-start.7 = (bf16[48,1152]{1,0:T(8,128)(2,1)S(1)}, bf16[48,1152]{1,0:T(8,128)(2,1)S(1)}, u32[]{:S(2)}, u32[]{:S(2)}) collective-permute-start(bf16[48,1152]{1,0:T(8,128)(2,1)S(1)} %shard_map.130.refs_0_), channel_id=1, source_target_pairs={{12,0},{14,2},{13,1},{15,3},{0,4},{2,6},{1,5},{3,7},{4,8},{6,10},{... | collective-permute-start | bytes 331784 | tf_op jit(solution)/shard_map/ppermute | solution.py:511
  17.2 10.4 %collective-permute-start.1 = (bf16[48,1152]{1,0:T(8,128)(2,1)S(1)}, bf16[48,1152]{1,0:T(8,128)(2,1)S(1)}, u32[]{:S(2)}, u32[]{:S(2)}) collective-permute-start(bf16[48,1152]{1,0:T(8,128)(2,1)S(1)} %shard_map.130.refs_0_), channel_id=1, source_target_pairs={{1,0},{3,2},{4,1},{6,3},{5,4},{7,6},{8,5},{10,7},{9,8},{11,10},{12... | collective-permute-start | bytes 331784 | tf_op jit(solution)/shard_map/ppermute | solution.py:511
  18.2 16.2 %copy-start.7 = (bf16[8,1152]{1,0:T(8,128)(2,1)}, bf16[8,1152]{1,0:T(8,128)(2,1)S(1)}, u32[]{:S(2)}) copy-start(bf16[8,1152]{1,0:T(8,128)(2,1)S(1)} %collective-permute-done.16.refs_17_.refs_4_) | copy-start | bytes 55300
  18.2 10.4 %collective-permute-start.3 = (bf16[48,1152]{1,0:T(8,128)(2,1)S(1)}, bf16[48,1152]{1,0:T(8,128)(2,1)S(1)}, u32[]{:S(2)}, u32[]{:S(2)}) collective-permute-start(bf16[48,1152]{1,0:T(8,128)(2,1)S(1)} %shard_map.130.refs_0_), channel_id=1, source_target_pairs={{13,0},{15,2},{0,1},{2,3},{1,4},{3,6},{4,5},{6,7},{5,8},{7,10},{8,... | collective-permute-start | bytes 331784 | tf_op jit(solution)/shard_map/ppermute | solution.py:511
  20.6 8.0 %collective-permute-start = (bf16[48,1152]{1,0:T(8,128)(2,1)S(1)}, bf16[48,1152]{1,0:T(8,128)(2,1)S(1)}, u32[]{:S(2)}, u32[]{:S(2)}) collective-permute-start(bf16[48,1152]{1,0:T(8,128)(2,1)S(1)} %shard_map.130.refs_0_), channel_id=1, source_target_pairs={{2,0},{0,2},{3,1},{1,3},{6,4},{4,6},{7,5},{5,7},{10,8},{8,10},{11,... | collective-permute-start | bytes 331784 | tf_op jit(solution)/shard_map/ppermute | solution.py:511
  21.0 8.1 %collective-permute-start.9 = (bf16[48,1152]{1,0:T(8,128)(2,1)S(1)}, bf16[48,1152]{1,0:T(8,128)(2,1)S(1)}, u32[]{:S(2)}, u32[]{:S(2)}) collective-permute-start(bf16[48,1152]{1,0:T(8,128)(2,1)S(1)} %collective-permute-done.5.refs_6_), channel_id=1, source_target_pairs={{1,0},{3,2},{4,1},{6,3},{5,4},{7,6},{8,5},{10,7},{9,8},{11,10},{12... | collective-permute-start | bytes 331784 | tf_op jit(solution)/shard_map/ppermute | solution.py:511
  26.4 6.1 %collective-permute-start.13 = (bf16[48,1152]{1,0:T(8,128)(2,1)S(1)}, bf16[48,1152]{1,0:T(8,128)(2,1)S(1)}, u32[]{:S(2)}, u32[]{:S(2)}) collective-permute-start(bf16[48,1152]{1,0:T(8,128)(2,1)S(1)} %collective-permute-done.5.refs_6_), channel_id=1, source_target_pairs={{4,0},{6,2},{5,1},{7,3},{8,4},{10,6},{9,5},{11,7},{12,8},{14,10},{... | collective-permute-start | bytes 331784 | tf_op jit(solution)/shard_map/ppermute | solution.py:511
  27.6 4.9 %collective-permute-start.11 = (bf16[48,1152]{1,0:T(8,128)(2,1)S(1)}, bf16[48,1152]{1,0:T(8,128)(2,1)S(1)}, u32[]{:S(2)}, u32[]{:S(2)}) collective-permute-start(bf16[48,1152]{1,0:T(8,128)(2,1)S(1)} %collective-permute-done.7.refs_8_), channel_id=1, source_target_pairs={{13,0},{15,2},{0,1},{2,3},{1,4},{3,6},{4,5},{6,7},{5,8},{7,10},{8,... | collective-permute-start | bytes 331784 | tf_op jit(solution)/shard_map/ppermute | solution.py:511
  28.6 4.4 %collective-permute-start.6 = (bf16[48,1152]{1,0:T(8,128)(2,1)S(1)}, bf16[48,1152]{1,0:T(8,128)(2,1)S(1)}, u32[]{:S(2)}, u32[]{:S(2)}) collective-permute-start(bf16[48,1152]{1,0:T(8,128)(2,1)S(1)} %collective-permute-done.5.refs_6_), channel_id=1, source_target_pairs={{2,0},{0,2},{3,1},{1,3},{6,4},{4,6},{7,5},{5,7},{10,8},{8,10},{11,... | collective-permute-start | bytes 331784 | tf_op jit(solution)/shard_map/ppermute | solution.py:511
  28.6 4.5 %collective-permute-start.8 = (bf16[48,1152]{1,0:T(8,128)(2,1)S(1)}, bf16[48,1152]{1,0:T(8,128)(2,1)S(1)}, u32[]{:S(2)}, u32[]{:S(2)}) collective-permute-start(bf16[48,1152]{1,0:T(8,128)(2,1)S(1)} %collective-permute-done.7.refs_8_), channel_id=1, source_target_pairs={{2,0},{0,2},{3,1},{1,3},{6,4},{4,6},{7,5},{5,7},{10,8},{8,10},{11,... | collective-permute-start | bytes 331784 | tf_op jit(solution)/shard_map/ppermute | solution.py:511
  29.1 4.4 %collective-permute-start.2 = (bf16[48,1152]{1,0:T(8,128)(2,1)S(1)}, bf16[48,1152]{1,0:T(8,128)(2,1)S(1)}, u32[]{:S(2)}, u32[]{:S(2)}) collective-permute-start(bf16[48,1152]{1,0:T(8,128)(2,1)S(1)} %collective-permute-done.1.refs_2_), channel_id=1, source_target_pairs={{2,0},{0,2},{3,1},{1,3},{6,4},{4,6},{7,5},{5,7},{10,8},{8,10},{11,... | collective-permute-start | bytes 331784 | tf_op jit(solution)/shard_map/ppermute | solution.py:511
  32.5 1.3 collective-permute-start.4
  32.5 1.5 %collective-permute-start.10 = (bf16[48,1152]{1,0:T(8,128)(2,1)S(1)}, bf16[48,1152]{1,0:T(8,128)(2,1)S(1)}, u32[]{:S(2)}, u32[]{:S(2)}) collective-permute-start(bf16[48,1152]{1,0:T(8,128)(2,1)S(1)} %collective-permute-done.9.refs_10_), channel_id=1, source_target_pairs={{2,0},{0,2},{3,1},{1,3},{6,4},{4,6},{7,5},{5,7},{10,8},{8,10},{11,... | collective-permute-start | bytes 331784 | tf_op jit(solution)/shard_map/ppermute | solution.py:511
  33.0 1.3 collective-permute-start.14
  33.1 1.4 collective-permute-start.12
  36.9 37.2 %collective-permute-start.17 = (bf16[5,48,1152]{2,1,0:T(8,128)(2,1)}, bf16[5,48,1152]{2,1,0:T(8,128)(2,1)S(1)}, u32[]{:S(2)}, u32[]{:S(2)}) collective-permute-start(bf16[5,48,1152]{2,1,0:T(8,128)(2,1)} %get-tuple-element.79), channel_id=1, source_target_pairs={{255,0},{254,1},{253,2},{252,3},{251,4},{250,5},{249,6},{248,7},{2... | collective-permute-start | bytes 1658888 | tf_op jit(solution)/shard_map/ppermute | solution.py:566
  45.3 28.7 %collective-permute-start.18 = (bf16[48,1152]{1,0:T(8,128)(2,1)}, bf16[48,1152]{1,0:T(8,128)(2,1)S(1)}, u32[]{:S(2)}, u32[]{:S(2)}) collective-permute-start(bf16[48,1152]{1,0:T(8,128)(2,1)} %get-tuple-element.80), channel_id=1, source_target_pairs={{15,0},{14,1},{13,2},{12,3},{11,4},{10,5},{9,6},{8,7},{7,8},{6,9},... | collective-permute-start | bytes 331784 | tf_op jit(solution)/shard_map/ppermute | solution.py:566
  74.1 26.7 %copy-start.2 = (bf16[2,4,128,192]{3,2,1,0:T(8,128)(2,1)S(1)}, bf16[2,4,128,192]{3,2,1,0:T(8,128)(2,1)}, u32[]{:S(2)}) copy-start(bf16[2,4,128,192]{3,2,1,0:T(8,128)(2,1)} %constant.81.clone.table_ref) | copy-start | bytes 1179652
  83.0 47.6 %copy-start = (bf16[1,1024,768]{2,1,0:T(8,128)(2,1)S(1)}, bf16[1,1024,768]{2,1,0:T(8,128)(2,1)}, u32[]{:S(2)}) copy-start(bf16[1,1024,768]{2,1,0:T(8,128)(2,1)} %constant.82.clone.tb_source) | copy-start | bytes 4718596
  83.0 47.5 %copy-start.1 = (bf16[2,640,384]{2,1,0:T(8,128)(2,1)S(1)}, bf16[2,640,384]{2,1,0:T(8,128)(2,1)}, u32[]{:S(2)}) copy-start(bf16[2,640,384]{2,1,0:T(8,128)(2,1)} %constant.83.clone.ta_source) | copy-start | bytes 2949124
  133.3 4.8 %collective-permute-start.19 = (bf16[48,1152]{1,0:T(8,128)(2,1)S(1)}, bf16[48,1152]{1,0:T(8,128)(2,1)S(1)}, u32[]{:S(2)}, u32[]{:S(2)}) collective-permute-start(bf16[48,1152]{1,0:T(8,128)(2,1)S(1)} %get-tuple-element.82), channel_id=1, source_target_pairs={{0,1},{1,0},{2,3},{3,2},{4,5},{5,4},{6,7},{7,6},{8,9},{9,8},{10,11... | collective-permute-start | bytes 331784 | tf_op jit(solution)/shard_map/ppermute | solution.py:632
  (4 other events, 24.0 us)

commit v3 on v1

--- a/solution.py
+++ b/solution.py
@@ -311,8 +311,7 @@
             raw[side * 3 + y, plane] = blocks[n, :, 384 * y : 384 * (y + 1)]
     for y in range(6):
         rows = raw[y].reshape(384, 384)
-        rows = (rows.astype(F32) * sign_ref[...]).astype(BF)
-        half[y] = dot_columns(rows, ta_ref).astype(BF)
+        half[y] = dot_columns(rows * sign_ref[...], ta_ref).astype(BF)
     for copy in copies[17:]:
         copy.wait()
     seconds = []
@@ -361,9 +360,11 @@
     sources[0] = sources[0].at[:, :, pl.ds(0, 4864)]
     copies = start_copies(sources, targets, arrival)
     eye_ref, flip_ref, order_ref, forward_ref, inverse_ref, in_ref = targets[count - 6 :]
-    for copy in copies[: count - 3]:
+    copies[0].wait()
+    copies[count - 6].wait()
+    own_weights(targets[0], eye_ref, weight, work)
+    for copy in copies[1 : count - 6] + copies[count - 5 : count - 3]:
         copy.wait()
-    own_weights(targets[0], eye_ref, weight, work)
     pair_weights(targets[1 : count - 6], flip_ref, order_ref, weight, work, held, rows)
     for copy in copies[count - 3 :]:
         copy.wait()
@@ -561,7 +562,7 @@
         g < lax.axis_size("gz"),
         spread,
         lambda *operands: jnp.zeros((16, 6, 16, 256), BF),
-        info, sign[None, :], *blocks, jnp.asarray(first_forward()), jnp.asarray(second_forward()),
+        info, sign[None, :].astype(BF), *blocks, jnp.asarray(first_forward()), jnp.asarray(second_forward()),
         jnp.asarray(third_forward()),
     )
     operands = (

time: 134 us -> 136 us (1.015)
  blocking collectives: 63.4 us -> 38.7 us
  waiting for transfers between devices: 12.5 us -> 25.8 us
  starting transfers between devices: 31.5 us -> 43.3 us
    all_to_all x1 -> x0, blocking collectives: 24.7 us -> none  [body(): lax.all_to_all(values, 'gz', split_axis=0, concat_axis=0, tiled=True)]
    all_to_all x0 -> x1, waiting for transfers between devices: none -> 13.9 us  [body(): lax.all_to_all(values, 'gz', split_axis=0, concat_axis=0, tiled=True)]
    all_to_all x0 -> x1, starting transfers between devices: none -> 11 us  [body(): lax.all_to_all(values, 'gz', split_axis=0, concat_axis=0, tiled=True)]
  transfers between devices with their start and end apart: 20 -> 21, of which waited for: 8 -> 9; matrix products, arithmetic and copies ran while one was open for 0% -> 0% of each run, Pallas kernels for 7% -> 6%
where the time goes in v3:
time: 136 us; the launch traced here: 134 us
  starting transfers between devices  43.3 us (32%)
  blocking collectives  38.7 us (28%)
  waiting for transfers between devices  25.8 us (19%)
  Pallas kernels  23.9 us (18%)
  local copies, waits for them, and re-layouts  2.41 us (2%)
    all_to_all x1, blocking collectives, body(): lax.all_to_all(values, 'ta', split_axis=0, concat_axis=0, tiled=True)  19.8 us
    all_to_all x1, blocking collectives, spread(): return lax.all_to_all(values, 'ta', split_axis=0, concat_axis=0, tiled=True)  18.9 us
    ppermute x4, starting transfers between devices, body(): lax.ppermute(s, AXES, mirror_pairs(*place))  15.5 us
    ppermute x15, starting transfers between devices, receive(): return lax.ppermute(values, AXES, column_pairs(shift, flip))  14.5 us
    all_to_all x1, waiting for transfers between devices, body(): lax.all_to_all(values, 'gz', split_axis=0, concat_axis=0, tiled=True)  13.9 us
    all_to_all x1, starting transfers between devices, body(): lax.all_to_all(values, 'gz', split_axis=0, concat_axis=0, tiled=True)  11 us
    ppermute x15, waiting for transfers between devices, receive(): return lax.ppermute(values, AXES, column_pairs(shift, flip))  9.12 us
    pallas_call x1, Pallas kernels, spread(): call(forward_kernel, shape((16, 6, 16, 256), BF), [pltpu.VMEM((6, 8, 48,...  8.67 us
  transfers between devices with their start and end apart: 21, of which 9 were waited for; matrix products, arithmetic and copies ran while one was open for 0% of the time, Pallas kernels for 6%

profile of v3, /device:TPU:32, one launch (start us, length us, event | category | flops | bytes accessed | tf_op | source)
XLA Modules:
  0.0 134.3 jit_solution(9083822622580526797)
XLA Ops:
  1.0 5.5 %collective-permute-start.5 = (bf16[48,1152]{1,0:T(8,128)(2,1)S(1)}, bf16[48,1152]{1,0:T(8,128)(2,1)S(1)}, u32[]{:S(2)}, u32[]{:S(2)}) collective-permute-start(bf16[48,1152]{1,0:T(8,128)(2,1)S(1)} %shard_map.130.refs_0_), channel_id=1, source_target_pairs={{4,0},{6,2},{5,1},{7,3},{8,4},{10,6},{9,5},{11,7},{12,8},{14,10},{... | collective-permute-start | bytes 331784 | tf_op jit(solution)/shard_map/ppermute | solution.py:501
  6.5 1.0 collective-permute-start.1
  7.5 1.0 collective-permute-start.3
  8.5 1.5 %collective-permute-done.5.refs_6_ = bf16[48,1152]{1,0:T(8,128)(2,1)S(1)} collective-permute-done((bf16[48,1152]{1,0:T(8,128)(2,1)S(1)}, bf16[48,1152]{1,0:T(8,128)(2,1)S(1)}, u32[]{:S(2)}, u32[]{:S(2)}) %collective-permute-start.5) | collective-permute-done | bytes 110624 | tf_op jit(solution)/shard_map/ppermute | solution.py:501
  10.0 2.9 %collective-permute-start.9 = (bf16[48,1152]{1,0:T(8,128)(2,1)S(1)}, bf16[48,1152]{1,0:T(8,128)(2,1)S(1)}, u32[]{:S(2)}, u32[]{:S(2)}) collective-permute-start(bf16[48,1152]{1,0:T(8,128)(2,1)S(1)} %collective-permute-done.5.refs_6_), channel_id=1, source_target_pairs={{1,0},{3,2},{4,1},{6,3},{5,4},{7,6},{8,5},{10,7},{9,8},{11,10},{12... | collective-permute-start | bytes 331784 | tf_op jit(solution)/shard_map/ppermute | solution.py:501
  12.9 3.0 %collective-permute-done.7.refs_8_ = bf16[48,1152]{1,0:T(8,128)(2,1)S(1)} collective-permute-done((bf16[48,1152]{1,0:T(8,128)(2,1)S(1)}, bf16[48,1152]{1,0:T(8,128)(2,1)S(1)}, u32[]{:S(2)}, u32[]{:S(2)}) %collective-permute-start.7) | collective-permute-done | bytes 110624 | tf_op jit(solution)/shard_map/ppermute | solution.py:501
  15.9 1.6 %collective-permute-start.13 = (bf16[48,1152]{1,0:T(8,128)(2,1)S(1)}, bf16[48,1152]{1,0:T(8,128)(2,1)S(1)}, u32[]{:S(2)}, u32[]{:S(2)}) collective-permute-start(bf16[48,1152]{1,0:T(8,128)(2,1)S(1)} %collective-permute-done.5.refs_6_), channel_id=1, source_target_pairs={{4,0},{6,2},{5,1},{7,3},{8,4},{10,6},{9,5},{11,7},{12,8},{14,10},{... | collective-permute-start | bytes 331784 | tf_op jit(solution)/shard_map/ppermute | solution.py:501
  19.1 3.6 %collective-permute-done.13.refs_14_ = bf16[48,1152]{1,0:T(8,128)(2,1)S(1)} collective-permute-done((bf16[48,1152]{1,0:T(8,128)(2,1)S(1)}, bf16[48,1152]{1,0:T(8,128)(2,1)S(1)}, u32[]{:S(2)}, u32[]{:S(2)}) %collective-permute-start.13) | collective-permute-done | bytes 110624 | tf_op jit(solution)/shard_map/ppermute | solution.py:501
  24.7 2.5 %shard_map.131 = (bf16[5,48,1152]{2,1,0:T(8,128)(2,1)}, bf16[48,1152]{1,0:T(8,128)(2,1)}, bf16[24,1152]{1,0:T(8,128)(2,1)}, bf16[8,1152]{1,0:T(8,128)(2,1)}) custom-call(f32[6,12,9216]{2,1,0:T(8,128)} %refs_0_.1, bf16[48,1152]{1,0:T(8,128)(2,1)S(1)} %shard_map.130.refs_0_, bf16[48,1152]{1,0:T(8,128)(2,1)S(1)} %collective-permute-done.refs_1_, ...), custom_call_target="tpu_custom_call" | custom-call | flops 100000000 | bytes 4000000 | tf_op jit(solution)/shard_map/pallas_call | solution.py:531
  27.2 7.4 %collective-permute-start.15 = (bf16[5,48,1152]{2,1,0:T(8,128)(2,1)}, bf16[5,48,1152]{2,1,0:T(8,128)(2,1)S(1)}, u32[]{:S(2)}, u32[]{:S(2)}) collective-permute-start(bf16[5,48,1152]{2,1,0:T(8,128)(2,1)} %get-tuple-element.77), channel_id=1, source_target_pairs={{255,0},{254,1},{253,2},{252,3},{251,4},{250,5},{249,6},{248,7},{2... | collective-permute-start | bytes 1658888 | tf_op jit(solution)/shard_map/ppermute | solution.py:541
  34.6 2.2 %collective-permute-start.16 = (bf16[48,1152]{1,0:T(8,128)(2,1)}, bf16[48,1152]{1,0:T(8,128)(2,1)S(1)}, u32[]{:S(2)}, u32[]{:S(2)}) collective-permute-start(bf16[48,1152]{1,0:T(8,128)(2,1)} %get-tuple-element.78), channel_id=1, source_target_pairs={{15,0},{14,1},{13,2},{12,3},{11,4},{10,5},{9,6},{8,7},{7,8},{6,9},... | collective-permute-start | bytes 331784 | tf_op jit(solution)/shard_map/ppermute | solution.py:541
  36.8 3.7 %collective-permute-start.17 = (bf16[24,1152]{1,0:T(8,128)(2,1)}, bf16[24,1152]{1,0:T(8,128)(2,1)S(1)}, u32[]{:S(2)}, u32[]{:S(2)}) collective-permute-start(bf16[24,1152]{1,0:T(8,128)(2,1)} %get-tuple-element.79), channel_id=1, source_target_pairs={{241,0},{240,1},{255,2},{254,3},{253,4},{252,5},{251,6},{250,7},{2... | collective-permute-start | bytes 165896 | tf_op jit(solution)/shard_map/ppermute | solution.py:541
  40.5 2.2 %collective-permute-start.18 = (bf16[8,1152]{1,0:T(8,128)(2,1)}, bf16[8,1152]{1,0:T(8,128)(2,1)S(1)}, u32[]{:S(2)}, u32[]{:S(2)}) collective-permute-start(bf16[8,1152]{1,0:T(8,128)(2,1)} %get-tuple-element.80), channel_id=1, source_target_pairs={{1,0},{0,1},{15,2},{14,3},{13,4},{12,5},{11,6},{10,7},{9,8},{8,9},... | collective-permute-start | bytes 55304 | tf_op jit(solution)/shard_map/ppermute | solution.py:541
  42.8 27.6 %conditional.1 = (bf16[16,6,16,256]{3,2,1,0:T(8,128)(2,1)S(1)}) conditional(s32[]{:T(128)} %convert_element_type.14, () %tuple.11, (s32[4]{0:T(128)S(1)}, bf16[1,384]{1,0:T(2,128)(2,1)S(1)}, bf16[48,1152]{1,0:T(8,128)(2,1)S(1)}, bf16[48,1152]{1,0:T(8,128)(2,1)S(1)}, bf16[48,1152]{1,0:T(8,128)(2,1)S(1)}, /*index=5*/bf16[48,1152]{1,0:T(8,128)(2,1)S(1)}, ...), branch_computations={%region_0.1_spmd, %region_1.2_spmd} | conditional | flops 100000000 | bytes 5572872 | solution.py:561
  42.8 8.7 %branch_1_fun.1 = bf16[16,6,16,256]{3,2,1,0:T(8,128)(2,1)} custom-call(s32[4]{0:T(128)S(1)} %get-tuple-element.50.info_ref, bf16[1,384]{1,0:T(2,128)(2,1)S(1)} %get-tuple-element.51.sign_ref, bf16[48,1152]{1,0:T(8,128)(2,1)S(1)} %get-tuple-element.52.refs_0_, bf16[48,1152]{1,0:T(8,128)(2,1)S(1)} %get-tuple-element.53.refs_1_, ...), custom_call_target="tpu_custom_call" | custom-call | flops 100000000 | bytes 4000000 | tf_op jit(solution)/shard_map/cond/branch_1_fun/pallas_call | solution.py:543
  51.4 18.9 %all_to_all.14 = bf16[16,6,16,256]{3,2,1,0:T(8,128)(2,1)S(1)} all-to-all(bf16[16,6,16,256]{3,2,1,0:T(8,128)(2,1)} %branch_1_fun.1), channel_id=1, replica_groups=mesh['ta'=16,'gz'=8,'gy'=2] {'ta'}, dimensions={0} | all-to-all | bytes 1572864 | tf_op jit(solution)/shard_map/cond/branch_1_fun/all_to_all | solution.py:559
  71.8 7.7 %shard_map.132 = bf16[16,6,16,256]{3,2,1,0:T(8,128)(2,1)} custom-call(f32[6,12,9216]{2,1,0:T(8,128)} %refs_0_.1, bf16[5,48,1152]{2,1,0:T(8,128)(2,1)} %copy-done.4, bf16[48,1152]{1,0:T(8,128)(2,1)} %copy-done.5, bf16[24,1152]{1,0:T(8,128)(2,1)} %copy-done.6, bf16[8,1152]{1,0:T(8,128)(2,1)} %copy-done.7, bf16[192,192]{1,0:T(8,128)(2,1)} %constant.76.clone.refs_5_, ...), custom_call_target="tpu_custom_call" | custom-call | flops 100000000 | bytes 4000000 | tf_op jit(solution)/shard_map/pallas_call | solution.py:572
  79.5 19.8 %all_to_all.15.in_ref = bf16[16,6,16,256]{3,2,1,0:T(8,128)(2,1)S(1)} all-to-all(bf16[16,6,16,256]{3,2,1,0:T(8,128)(2,1)} %shard_map.132), channel_id=1, replica_groups=mesh['ta'=16,'gz'=8,'gy'=2] {'ta'}, dimensions={0} | all-to-all | bytes 1572864 | tf_op jit(solution)/shard_map/all_to_all | solution.py:587
  99.4 1.6 %shard_map.133 = bf16[8,6,16,256]{3,2,1,0:T(8,128)(2,1)} custom-call(bf16[16,6,16,256]{3,2,1,0:T(8,128)(2,1)S(1)} %all_to_all.15.in_ref, bf16[2,4,128,192]{3,2,1,0:T(8,128)(2,1)S(1)} %copy-done.2), custom_call_target="tpu_custom_call" | custom-call | flops 100000000 | bytes 4000000 | tf_op jit(solution)/shard_map/pallas_call | solution.py:588
  100.9 11.0 %all-to-all-start.2 = ((bf16[8,6,16,256]{3,2,1,0:T(8,128)(2,1)}), bf16[8,6,16,256]{3,2,1,0:T(8,128)(2,1)S(1)}, u32[]{:S(2)}, u32[]{:S(2)}) async-start(bf16[8,6,16,256]{3,2,1,0:T(8,128)(2,1)} %shard_map.133), calls=%async_computation.2 | async-start | bytes 786432 | tf_op jit(solution)/shard_map/all_to_all | solution.py:591
  111.9 13.9 %all-to-all-done.2.in_ref = bf16[8,6,16,256]{3,2,1,0:T(8,128)(2,1)S(1)} async-done(((bf16[8,6,16,256]{3,2,1,0:T(8,128)(2,1)}), bf16[8,6,16,256]{3,2,1,0:T(8,128)(2,1)S(1)}, u32[]{:S(2)}, u32[]{:S(2)}) %all-to-all-start.2) | async-done | bytes 393248 | tf_op jit(solution)/shard_map/all_to_all | solution.py:591
  125.8 2.7 %shard_map.134 = (f32[6,6,1152]{2,1,0:T(8,128)S(1)}, bf16[48,1152]{1,0:T(8,128)(2,1)S(1)}) custom-call(s32[4]{0:T(128)S(1)} %pad_add_fusion.info_ref, bf16[8,6,16,256]{3,2,1,0:T(8,128)(2,1)S(1)} %all-to-all-done.2.in_ref, bf16[1,1024,768]{2,1,0:T(8,128)(2,1)S(1)} %copy-done, bf16[2,640,384]{2,1,0:T(8,128)(2,1)S(1)} %copy-done.1, ...), custom_call_target="tpu_custom_call" | custom-call | flops 100000000 | bytes 4000000 | tf_op jit(solution)/shard_map/pallas_call | solution.py:592
  128.6 2.3 %collective-permute-start.19 = (bf16[48,1152]{1,0:T(8,128)(2,1)S(1)}, bf16[48,1152]{1,0:T(8,128)(2,1)S(1)}, u32[]{:S(2)}, u32[]{:S(2)}) collective-permute-start(bf16[48,1152]{1,0:T(8,128)(2,1)S(1)} %get-tuple-element.82), channel_id=1, source_target_pairs={{0,1},{1,0},{2,3},{3,2},{4,5},{5,4},{6,7},{7,6},{8,9},{9,8},{10,11... | collective-permute-start | bytes 331784 | tf_op jit(solution)/shard_map/ppermute | solution.py:605
  130.8 2.7 %collective-permute-done.19.other_ref = bf16[48,1152]{1,0:T(8,128)(2,1)S(1)} collective-permute-done((bf16[48,1152]{1,0:T(8,128)(2,1)S(1)}, bf16[48,1152]{1,0:T(8,128)(2,1)S(1)}, u32[]{:S(2)}, u32[]{:S(2)}) %collective-permute-start.19) | collective-permute-done | bytes 110624 | tf_op jit(solution)/shard_map/ppermute | solution.py:605
  (47 shorter events, 6.8 us)
Async XLA Ops:
  1.0 9.0 %collective-permute-start.5 = (bf16[48,1152]{1,0:T(8,128)(2,1)S(1)}, bf16[48,1152]{1,0:T(8,128)(2,1)S(1)}, u32[]{:S(2)}, u32[]{:S(2)}) collective-permute-start(bf16[48,1152]{1,0:T(8,128)(2,1)S(1)} %shard_map.130.refs_0_), channel_id=1, source_target_pairs={{4,0},{6,2},{5,1},{7,3},{8,4},{10,6},{9,5},{11,7},{12,8},{14,10},{... | collective-permute-start | bytes 331784 | tf_op jit(solution)/shard_map/ppermute | solution.py:501
  6.5 9.5 %collective-permute-start.7 = (bf16[48,1152]{1,0:T(8,128)(2,1)S(1)}, bf16[48,1152]{1,0:T(8,128)(2,1)S(1)}, u32[]{:S(2)}, u32[]{:S(2)}) collective-permute-start(bf16[48,1152]{1,0:T(8,128)(2,1)S(1)} %shard_map.130.refs_0_), channel_id=1, source_target_pairs={{12,0},{14,2},{13,1},{15,3},{0,4},{2,6},{1,5},{3,7},{4,8},{6,10},{... | collective-permute-start | bytes 331784 | tf_op jit(solution)/shard_map/ppermute | solution.py:501
  6.5 11.1 %collective-permute-start.1 = (bf16[48,1152]{1,0:T(8,128)(2,1)S(1)}, bf16[48,1152]{1,0:T(8,128)(2,1)S(1)}, u32[]{:S(2)}, u32[]{:S(2)}) collective-permute-start(bf16[48,1152]{1,0:T(8,128)(2,1)S(1)} %shard_map.130.refs_0_), channel_id=1, source_target_pairs={{1,0},{3,2},{4,1},{6,3},{5,4},{7,6},{8,5},{10,7},{9,8},{11,10},{12... | collective-permute-start | bytes 331784 | tf_op jit(solution)/shard_map/ppermute | solution.py:501
  7.5 11.0 %collective-permute-start.3 = (bf16[48,1152]{1,0:T(8,128)(2,1)S(1)}, bf16[48,1152]{1,0:T(8,128)(2,1)S(1)}, u32[]{:S(2)}, u32[]{:S(2)}) collective-permute-start(bf16[48,1152]{1,0:T(8,128)(2,1)S(1)} %shard_map.130.refs_0_), channel_id=1, source_target_pairs={{13,0},{15,2},{0,1},{2,3},{1,4},{3,6},{4,5},{6,7},{5,8},{7,10},{8,... | collective-permute-start | bytes 331784 | tf_op jit(solution)/shard_map/ppermute | solution.py:501
  8.5 10.0 %collective-permute-start = (bf16[48,1152]{1,0:T(8,128)(2,1)S(1)}, bf16[48,1152]{1,0:T(8,128)(2,1)S(1)}, u32[]{:S(2)}, u32[]{:S(2)}) collective-permute-start(bf16[48,1152]{1,0:T(8,128)(2,1)S(1)} %shard_map.130.refs_0_), channel_id=1, source_target_pairs={{2,0},{0,2},{3,1},{1,3},{6,4},{4,6},{7,5},{5,7},{10,8},{8,10},{11,... | collective-permute-start | bytes 331784 | tf_op jit(solution)/shard_map/ppermute | solution.py:501
  10.0 9.0 %collective-permute-start.9 = (bf16[48,1152]{1,0:T(8,128)(2,1)S(1)}, bf16[48,1152]{1,0:T(8,128)(2,1)S(1)}, u32[]{:S(2)}, u32[]{:S(2)}) collective-permute-start(bf16[48,1152]{1,0:T(8,128)(2,1)S(1)} %collective-permute-done.5.refs_6_), channel_id=1, source_target_pairs={{1,0},{3,2},{4,1},{6,3},{5,4},{7,6},{8,5},{10,7},{9,8},{11,10},{12... | collective-permute-start | bytes 331784 | tf_op jit(solution)/shard_map/ppermute | solution.py:501
  15.9 6.7 %collective-permute-start.13 = (bf16[48,1152]{1,0:T(8,128)(2,1)S(1)}, bf16[48,1152]{1,0:T(8,128)(2,1)S(1)}, u32[]{:S(2)}, u32[]{:S(2)}) collective-permute-start(bf16[48,1152]{1,0:T(8,128)(2,1)S(1)} %collective-permute-done.5.refs_6_), channel_id=1, source_target_pairs={{4,0},{6,2},{5,1},{7,3},{8,4},{10,6},{9,5},{11,7},{12,8},{14,10},{... | collective-permute-start | bytes 331784 | tf_op jit(solution)/shard_map/ppermute | solution.py:501
  17.5 5.2 %collective-permute-start.11 = (bf16[48,1152]{1,0:T(8,128)(2,1)S(1)}, bf16[48,1152]{1,0:T(8,128)(2,1)S(1)}, u32[]{:S(2)}, u32[]{:S(2)}) collective-permute-start(bf16[48,1152]{1,0:T(8,128)(2,1)S(1)} %collective-permute-done.7.refs_8_), channel_id=1, source_target_pairs={{13,0},{15,2},{0,1},{2,3},{1,4},{3,6},{4,5},{6,7},{5,8},{7,10},{8,... | collective-permute-start | bytes 331784 | tf_op jit(solution)/shard_map/ppermute | solution.py:501
  18.5 4.7 %collective-permute-start.6 = (bf16[48,1152]{1,0:T(8,128)(2,1)S(1)}, bf16[48,1152]{1,0:T(8,128)(2,1)S(1)}, u32[]{:S(2)}, u32[]{:S(2)}) collective-permute-start(bf16[48,1152]{1,0:T(8,128)(2,1)S(1)} %collective-permute-done.5.refs_6_), channel_id=1, source_target_pairs={{2,0},{0,2},{3,1},{1,3},{6,4},{4,6},{7,5},{5,7},{10,8},{8,10},{11,... | collective-permute-start | bytes 331784 | tf_op jit(solution)/shard_map/ppermute | solution.py:501
  18.5 4.8 %collective-permute-start.8 = (bf16[48,1152]{1,0:T(8,128)(2,1)S(1)}, bf16[48,1152]{1,0:T(8,128)(2,1)S(1)}, u32[]{:S(2)}, u32[]{:S(2)}) collective-permute-start(bf16[48,1152]{1,0:T(8,128)(2,1)S(1)} %collective-permute-done.7.refs_8_), channel_id=1, source_target_pairs={{2,0},{0,2},{3,1},{1,3},{6,4},{4,6},{7,5},{5,7},{10,8},{8,10},{11,... | collective-permute-start | bytes 331784 | tf_op jit(solution)/shard_map/ppermute | solution.py:501
  19.0 4.7 %collective-permute-start.2 = (bf16[48,1152]{1,0:T(8,128)(2,1)S(1)}, bf16[48,1152]{1,0:T(8,128)(2,1)S(1)}, u32[]{:S(2)}, u32[]{:S(2)}) collective-permute-start(bf16[48,1152]{1,0:T(8,128)(2,1)S(1)} %collective-permute-done.1.refs_2_), channel_id=1, source_target_pairs={{2,0},{0,2},{3,1},{1,3},{6,4},{4,6},{7,5},{5,7},{10,8},{8,10},{11,... | collective-permute-start | bytes 331784 | tf_op jit(solution)/shard_map/ppermute | solution.py:501
  22.7 1.3 collective-permute-start.4
  22.7 1.5 %collective-permute-start.10 = (bf16[48,1152]{1,0:T(8,128)(2,1)S(1)}, bf16[48,1152]{1,0:T(8,128)(2,1)S(1)}, u32[]{:S(2)}, u32[]{:S(2)}) collective-permute-start(bf16[48,1152]{1,0:T(8,128)(2,1)S(1)} %collective-permute-done.9.refs_10_), channel_id=1, source_target_pairs={{2,0},{0,2},{3,1},{1,3},{6,4},{4,6},{7,5},{5,7},{10,8},{8,10},{11,... | collective-permute-start | bytes 331784 | tf_op jit(solution)/shard_map/ppermute | solution.py:501
  23.2 1.3 collective-permute-start.14
  23.3 1.4 %collective-permute-start.12 = (bf16[48,1152]{1,0:T(8,128)(2,1)S(1)}, bf16[48,1152]{1,0:T(8,128)(2,1)S(1)}, u32[]{:S(2)}, u32[]{:S(2)}) collective-permute-start(bf16[48,1152]{1,0:T(8,128)(2,1)S(1)} %collective-permute-done.11.refs_12_), channel_id=1, source_target_pairs={{2,0},{0,2},{3,1},{1,3},{6,4},{4,6},{7,5},{5,7},{10,8},{8,10},{11,... | collective-permute-start | bytes 331784 | tf_op jit(solution)/shard_map/ppermute | solution.py:501
  27.2 43.2 %collective-permute-start.15 = (bf16[5,48,1152]{2,1,0:T(8,128)(2,1)}, bf16[5,48,1152]{2,1,0:T(8,128)(2,1)S(1)}, u32[]{:S(2)}, u32[]{:S(2)}) collective-permute-start(bf16[5,48,1152]{2,1,0:T(8,128)(2,1)} %get-tuple-element.77), channel_id=1, source_target_pairs={{255,0},{254,1},{253,2},{252,3},{251,4},{250,5},{249,6},{248,7},{2... | collective-permute-start | bytes 1658888 | tf_op jit(solution)/shard_map/ppermute | solution.py:541
  34.6 35.8 %collective-permute-start.16 = (bf16[48,1152]{1,0:T(8,128)(2,1)}, bf16[48,1152]{1,0:T(8,128)(2,1)S(1)}, u32[]{:S(2)}, u32[]{:S(2)}) collective-permute-start(bf16[48,1152]{1,0:T(8,128)(2,1)} %get-tuple-element.78), channel_id=1, source_target_pairs={{15,0},{14,1},{13,2},{12,3},{11,4},{10,5},{9,6},{8,7},{7,8},{6,9},... | collective-permute-start | bytes 331784 | tf_op jit(solution)/shard_map/ppermute | solution.py:541
  36.8 33.5 %collective-permute-start.17 = (bf16[24,1152]{1,0:T(8,128)(2,1)}, bf16[24,1152]{1,0:T(8,128)(2,1)S(1)}, u32[]{:S(2)}, u32[]{:S(2)}) collective-permute-start(bf16[24,1152]{1,0:T(8,128)(2,1)} %get-tuple-element.79), channel_id=1, source_target_pairs={{241,0},{240,1},{255,2},{254,3},{253,4},{252,5},{251,6},{250,7},{2... | collective-permute-start | bytes 165896 | tf_op jit(solution)/shard_map/ppermute | solution.py:541
  40.5 29.9 %collective-permute-start.18 = (bf16[8,1152]{1,0:T(8,128)(2,1)}, bf16[8,1152]{1,0:T(8,128)(2,1)S(1)}, u32[]{:S(2)}, u32[]{:S(2)}) collective-permute-start(bf16[8,1152]{1,0:T(8,128)(2,1)} %get-tuple-element.80), channel_id=1, source_target_pairs={{1,0},{0,1},{15,2},{14,3},{13,4},{12,5},{11,6},{10,7},{9,8},{8,9},... | collective-permute-start | bytes 55304 | tf_op jit(solution)/shard_map/ppermute | solution.py:541
  70.3 29.0 %copy-start.2 = (bf16[2,4,128,192]{3,2,1,0:T(8,128)(2,1)S(1)}, bf16[2,4,128,192]{3,2,1,0:T(8,128)(2,1)}, u32[]{:S(2)}) copy-start(bf16[2,4,128,192]{3,2,1,0:T(8,128)(2,1)} %constant.81.clone.table_ref) | copy-start | bytes 1179652
  79.5 46.3 %copy-start = (bf16[1,1024,768]{2,1,0:T(8,128)(2,1)S(1)}, bf16[1,1024,768]{2,1,0:T(8,128)(2,1)}, u32[]{:S(2)}) copy-start(bf16[1,1024,768]{2,1,0:T(8,128)(2,1)} %constant.82.clone.tb_source) | copy-start | bytes 4718596
  79.5 46.3 %copy-start.1 = (bf16[2,640,384]{2,1,0:T(8,128)(2,1)S(1)}, bf16[2,640,384]{2,1,0:T(8,128)(2,1)}, u32[]{:S(2)}) copy-start(bf16[2,640,384]{2,1,0:T(8,128)(2,1)} %constant.83.clone.ta_source) | copy-start | bytes 2949124
  100.9 24.9 %all-to-all-start.2 = ((bf16[8,6,16,256]{3,2,1,0:T(8,128)(2,1)}), bf16[8,6,16,256]{3,2,1,0:T(8,128)(2,1)S(1)}, u32[]{:S(2)}, u32[]{:S(2)}) async-start(bf16[8,6,16,256]{3,2,1,0:T(8,128)(2,1)} %shard_map.133), calls=%async_computation.2 | async-start | bytes 786432 | tf_op jit(solution)/shard_map/all_to_all | solution.py:591
  128.6 5.0 %collective-permute-start.19 = (bf16[48,1152]{1,0:T(8,128)(2,1)S(1)}, bf16[48,1152]{1,0:T(8,128)(2,1)S(1)}, u32[]{:S(2)}, u32[]{:S(2)}) collective-permute-start(bf16[48,1152]{1,0:T(8,128)(2,1)S(1)} %get-tuple-element.82), channel_id=1, source_target_pairs={{0,1},{1,0},{2,3},{3,2},{4,5},{5,4},{6,7},{7,6},{8,9},{9,8},{10,11... | collective-permute-start | bytes 331784 | tf_op jit(solution)/shard_map/ppermute | solution.py:605
  (5 other events, 3.6 us)

commit v4 on v1

--- a/solution.py
+++ b/solution.py
@@ -416,10 +416,8 @@
 
 
 def last_kernel(
-    info_ref, in_ref, tb_source, ta_source, sign_ref, own_ref, send_ref, work, spare, both,
-    tb_ref, ta_ref, arrival
+    info_ref, in_ref, tb_ref, ta_ref, sign_ref, own_ref, send_ref, work, spare, both
 ):
-    copies = start_copies((tb_source, ta_source), (tb_ref, ta_ref), arrival)
     side = info_ref[2]
     values = in_ref[...].astype(F32).reshape(768, 256)
     work[0] = values[:, :128]
@@ -446,8 +444,6 @@
         imag_tile = shaped_spare[g, :, 1].reshape(48, 128)
         groups[4].append(jnp.where(low, real_tile, swap_half(imag_tile)))
     rows = jnp.concatenate([jnp.concatenate(group, axis=1) for group in groups], axis=0).astype(BF)
-    for copy in copies:
-        copy.wait()
     half = dot_columns(rows, tb_ref).astype(BF)
     rows = jnp.concatenate(
         [
@@ -595,11 +591,8 @@
             pltpu.VMEM((2, 768, 128), F32),
             pltpu.VMEM((768, 128), F32),
             pltpu.VMEM((2, 48, 1152), F32),
-            pltpu.VMEM((1, 1024, 768), BF),
-            pltpu.VMEM((2, 640, 384), BF),
-            pltpu.SemaphoreType.DMA((2,)),
         ],
-        in_specs=[smem_spec(), vmem_spec(), anywhere, anywhere, vmem_spec()],
+        in_specs=[smem_spec()] + [vmem_spec()] * 4,
     )(info, values, jnp.asarray(second_inverse()), jnp.asarray(first_inverse()), sign[None, :])
     other = lax.ppermute(send, "gy", [(0, 1), (1, 0)])
     return call(sum_kernel, shape((6, 6, 1152), F32), vmem=8)(own, other)

time: 134 us -> 134 us (level)
  no operation moved by 1% of the time
where the time goes in v4:
time: 134 us; the launch traced here: 132 us
  blocking collectives  63.4 us (47%)
  starting transfers between devices  31.5 us (24%)
  Pallas kernels  22.4 us (17%)
  waiting for transfers between devices  12.5 us (9%)
  local copies, waits for them, and re-layouts  2.41 us (2%)
    all_to_all x1, blocking collectives, body(): lax.all_to_all(values, 'gz', split_axis=0, concat_axis=0, tiled=True)  24.7 us
    all_to_all x1, blocking collectives, body(): lax.all_to_all(values, 'ta', split_axis=0, concat_axis=0, tiled=True)  19.8 us
    all_to_all x1, blocking collectives, spread(): return lax.all_to_all(values, 'ta', split_axis=0, concat_axis=0, tiled=True)  18.9 us
    ppermute x4, starting transfers between devices, body(): lax.ppermute(s, AXES, mirror_pairs(*place))  15.5 us
    ppermute x15, starting transfers between devices, receive(): return lax.ppermute(values, AXES, column_pairs(shift, flip))  14.5 us
    ppermute x15, waiting for transfers between devices, receive(): return lax.ppermute(values, AXES, column_pairs(shift, flip))  9.12 us
    pallas_call x1, Pallas kernels, spread(): call(forward_kernel, shape((16, 6, 16, 256), BF), [pltpu.VMEM((6, 8, 48,...  8.66 us
    pallas_call x1, Pallas kernels, body(): call(time_kernel, shape((16, 6, 16, 256), BF), [pltpu.VMEM((6, 12, 4864),...  7.46 us
  transfers between devices with their start and end apart: 20, of which 8 were waited for; matrix products, arithmetic and copies ran while one was open for 0% of the time, Pallas kernels for 7%

profile of v4, /device:TPU:32, one launch (start us, length us, event | category | flops | bytes accessed | tf_op | source)
XLA Modules:
  0.0 132.4 jit_solution(8976267235410425629)
XLA Ops:
  0.0 0.9 copy-done.3
  1.0 5.5 %collective-permute-start.5 = (bf16[48,1152]{1,0:T(8,128)(2,1)S(1)}, bf16[48,1152]{1,0:T(8,128)(2,1)S(1)}, u32[]{:S(2)}, u32[]{:S(2)}) collective-permute-start(bf16[48,1152]{1,0:T(8,128)(2,1)S(1)} %shard_map.130.refs_0_), channel_id=1, source_target_pairs={{4,0},{6,2},{5,1},{7,3},{8,4},{10,6},{9,5},{11,7},{12,8},{14,10},{... | collective-permute-start | bytes 331784 | tf_op jit(solution)/shard_map/ppermute | solution.py:496
  6.5 1.0 collective-permute-start.1
  7.5 1.0 collective-permute-start.3
  8.5 1.5 %collective-permute-done.5.refs_6_ = bf16[48,1152]{1,0:T(8,128)(2,1)S(1)} collective-permute-done((bf16[48,1152]{1,0:T(8,128)(2,1)S(1)}, bf16[48,1152]{1,0:T(8,128)(2,1)S(1)}, u32[]{:S(2)}, u32[]{:S(2)}) %collective-permute-start.5) | collective-permute-done | bytes 110624 | tf_op jit(solution)/shard_map/ppermute | solution.py:496
  10.0 2.9 %collective-permute-start.9 = (bf16[48,1152]{1,0:T(8,128)(2,1)S(1)}, bf16[48,1152]{1,0:T(8,128)(2,1)S(1)}, u32[]{:S(2)}, u32[]{:S(2)}) collective-permute-start(bf16[48,1152]{1,0:T(8,128)(2,1)S(1)} %collective-permute-done.5.refs_6_), channel_id=1, source_target_pairs={{1,0},{3,2},{4,1},{6,3},{5,4},{7,6},{8,5},{10,7},{9,8},{11,10},{12... | collective-permute-start | bytes 331784 | tf_op jit(solution)/shard_map/ppermute | solution.py:496
  12.9 3.0 %collective-permute-done.7.refs_8_ = bf16[48,1152]{1,0:T(8,128)(2,1)S(1)} collective-permute-done((bf16[48,1152]{1,0:T(8,128)(2,1)S(1)}, bf16[48,1152]{1,0:T(8,128)(2,1)S(1)}, u32[]{:S(2)}, u32[]{:S(2)}) %collective-permute-start.7) | collective-permute-done | bytes 110624 | tf_op jit(solution)/shard_map/ppermute | solution.py:496
  15.9 1.6 %collective-permute-start.13 = (bf16[48,1152]{1,0:T(8,128)(2,1)S(1)}, bf16[48,1152]{1,0:T(8,128)(2,1)S(1)}, u32[]{:S(2)}, u32[]{:S(2)}) collective-permute-start(bf16[48,1152]{1,0:T(8,128)(2,1)S(1)} %collective-permute-done.5.refs_6_), channel_id=1, source_target_pairs={{4,0},{6,2},{5,1},{7,3},{8,4},{10,6},{9,5},{11,7},{12,8},{14,10},{... | collective-permute-start | bytes 331784 | tf_op jit(solution)/shard_map/ppermute | solution.py:496
  17.5 0.9 collective-permute-start.11
  19.1 3.6 %collective-permute-done.13.refs_14_ = bf16[48,1152]{1,0:T(8,128)(2,1)S(1)} collective-permute-done((bf16[48,1152]{1,0:T(8,128)(2,1)S(1)}, bf16[48,1152]{1,0:T(8,128)(2,1)S(1)}, u32[]{:S(2)}, u32[]{:S(2)}) %collective-permute-start.13) | collective-permute-done | bytes 110624 | tf_op jit(solution)/shard_map/ppermute | solution.py:496
  24.7 2.5 %shard_map.131 = (bf16[5,48,1152]{2,1,0:T(8,128)(2,1)}, bf16[48,1152]{1,0:T(8,128)(2,1)}, bf16[24,1152]{1,0:T(8,128)(2,1)}, bf16[8,1152]{1,0:T(8,128)(2,1)}) custom-call(f32[6,12,9216]{2,1,0:T(8,128)} %refs_0_.1, bf16[48,1152]{1,0:T(8,128)(2,1)S(1)} %shard_map.130.refs_0_, bf16[48,1152]{1,0:T(8,128)(2,1)S(1)} %collective-permute-done.refs_1_, ...), custom_call_target="tpu_custom_call" | custom-call | flops 100000000 | bytes 4000000 | tf_op jit(solution)/shard_map/pallas_call | solution.py:526
  27.2 7.4 %collective-permute-start.15 = (bf16[5,48,1152]{2,1,0:T(8,128)(2,1)}, bf16[5,48,1152]{2,1,0:T(8,128)(2,1)S(1)}, u32[]{:S(2)}, u32[]{:S(2)}) collective-permute-start(bf16[5,48,1152]{2,1,0:T(8,128)(2,1)} %get-tuple-element.77), channel_id=1, source_target_pairs={{255,0},{254,1},{253,2},{252,3},{251,4},{250,5},{249,6},{248,7},{2... | collective-permute-start | bytes 1658888 | tf_op jit(solution)/shard_map/ppermute | solution.py:536
  34.6 2.2 %collective-permute-start.16 = (bf16[48,1152]{1,0:T(8,128)(2,1)}, bf16[48,1152]{1,0:T(8,128)(2,1)S(1)}, u32[]{:S(2)}, u32[]{:S(2)}) collective-permute-start(bf16[48,1152]{1,0:T(8,128)(2,1)} %get-tuple-element.78), channel_id=1, source_target_pairs={{15,0},{14,1},{13,2},{12,3},{11,4},{10,5},{9,6},{8,7},{7,8},{6,9},... | collective-permute-start | bytes 331784 | tf_op jit(solution)/shard_map/ppermute | solution.py:536
  36.8 3.7 %collective-permute-start.17 = (bf16[24,1152]{1,0:T(8,128)(2,1)}, bf16[24,1152]{1,0:T(8,128)(2,1)S(1)}, u32[]{:S(2)}, u32[]{:S(2)}) collective-permute-start(bf16[24,1152]{1,0:T(8,128)(2,1)} %get-tuple-element.79), channel_id=1, source_target_pairs={{241,0},{240,1},{255,2},{254,3},{253,4},{252,5},{251,6},{250,7},{2... | collective-permute-start | bytes 165896 | tf_op jit(solution)/shard_map/ppermute | solution.py:536
  40.4 2.2 %collective-permute-start.18 = (bf16[8,1152]{1,0:T(8,128)(2,1)}, bf16[8,1152]{1,0:T(8,128)(2,1)S(1)}, u32[]{:S(2)}, u32[]{:S(2)}) collective-permute-start(bf16[8,1152]{1,0:T(8,128)(2,1)} %get-tuple-element.80), channel_id=1, source_target_pairs={{1,0},{0,1},{15,2},{14,3},{13,4},{12,5},{11,6},{10,7},{9,8},{8,9},... | collective-permute-start | bytes 55304 | tf_op jit(solution)/shard_map/ppermute | solution.py:536
  42.7 27.5 %conditional.1 = (bf16[16,6,16,256]{3,2,1,0:T(8,128)(2,1)S(1)}) conditional(s32[]{:T(128)} %convert_element_type.3, () %tuple.11, (s32[4]{0:T(128)S(1)}, f32[1,384]{1,0:T(1,128)S(1)}, bf16[48,1152]{1,0:T(8,128)(2,1)S(1)}, bf16[48,1152]{1,0:T(8,128)(2,1)S(1)}, bf16[48,1152]{1,0:T(8,128)(2,1)S(1)}, /*index=5*/bf16[48,1152]{1,0:T(8,128)(2,1)S(1)}, ...), branch_computations={%region_0.1_spmd, %region_1.2_spmd} | conditional | flops 100000000 | bytes 5572872 | solution.py:556
  42.7 8.7 %branch_1_fun.1 = bf16[16,6,16,256]{3,2,1,0:T(8,128)(2,1)} custom-call(s32[4]{0:T(128)S(1)} %get-tuple-element.50.info_ref, f32[1,384]{1,0:T(1,128)S(1)} %get-tuple-element.51.sign_ref, bf16[48,1152]{1,0:T(8,128)(2,1)S(1)} %get-tuple-element.52.refs_0_, bf16[48,1152]{1,0:T(8,128)(2,1)S(1)} %get-tuple-element.53.refs_1_, ...), custom_call_target="tpu_custom_call" | custom-call | flops 100000000 | bytes 4000000 | tf_op jit(solution)/shard_map/cond/branch_1_fun/pallas_call | solution.py:538
  51.4 18.9 %all_to_all.14 = bf16[16,6,16,256]{3,2,1,0:T(8,128)(2,1)S(1)} all-to-all(bf16[16,6,16,256]{3,2,1,0:T(8,128)(2,1)} %branch_1_fun.1), channel_id=1, replica_groups=mesh['ta'=16,'gz'=8,'gy'=2] {'ta'}, dimensions={0} | all-to-all | bytes 1572864 | tf_op jit(solution)/shard_map/cond/branch_1_fun/all_to_all | solution.py:554
  71.8 7.5 %shard_map.132 = bf16[16,6,16,256]{3,2,1,0:T(8,128)(2,1)} custom-call(f32[6,12,9216]{2,1,0:T(8,128)} %refs_0_.1, bf16[5,48,1152]{2,1,0:T(8,128)(2,1)} %copy-done.4, bf16[48,1152]{1,0:T(8,128)(2,1)} %copy-done.5, bf16[24,1152]{1,0:T(8,128)(2,1)} %copy-done.6, bf16[8,1152]{1,0:T(8,128)(2,1)} %copy-done.7, bf16[192,192]{1,0:T(8,128)(2,1)} %constant.76.clone.refs_5_, ...), custom_call_target="tpu_custom_call" | custom-call | flops 100000000 | bytes 4000000 | tf_op jit(solution)/shard_map/pallas_call | solution.py:567
  79.3 19.8 %all_to_all.15.in_ref = bf16[16,6,16,256]{3,2,1,0:T(8,128)(2,1)S(1)} all-to-all(bf16[16,6,16,256]{3,2,1,0:T(8,128)(2,1)} %shard_map.132), channel_id=1, replica_groups=mesh['ta'=16,'gz'=8,'gy'=2] {'ta'}, dimensions={0} | all-to-all | bytes 1572864 | tf_op jit(solution)/shard_map/all_to_all | solution.py:582
  100.0 24.7 %all_to_all.16.in_ref = bf16[8,6,16,256]{3,2,1,0:T(8,128)(2,1)S(1)} all-to-all(bf16[8,6,16,256]{3,2,1,0:T(8,128)(2,1)S(1)} %shard_map.133), channel_id=1, replica_groups=mesh['ta'=16,'gz'=8,'gy'=2] {'gz'}, dimensions={0} | all-to-all | bytes 786432 | tf_op jit(solution)/shard_map/all_to_all | solution.py:586
  124.7 2.2 %shard_map.134 = (f32[6,6,1152]{2,1,0:T(8,128)S(1)}, bf16[48,1152]{1,0:T(8,128)(2,1)S(1)}) custom-call(s32[4]{0:T(128)S(1)} %pad_add_fusion.info_ref, bf16[8,6,16,256]{3,2,1,0:T(8,128)(2,1)S(1)} %all_to_all.16.in_ref, bf16[1,1024,768]{2,1,0:T(8,128)(2,1)S(1)} %copy-done, bf16[2,640,384]{2,1,0:T(8,128)(2,1)S(1)} %copy-done.1, ...), custom_call_target="tpu_custom_call" | custom-call | flops 100000000 | bytes 4000000 | tf_op jit(solution)/shard_map/pallas_call | solution.py:587
  126.9 1.4 %collective-permute-start.19 = (bf16[48,1152]{1,0:T(8,128)(2,1)S(1)}, bf16[48,1152]{1,0:T(8,128)(2,1)S(1)}, u32[]{:S(2)}, u32[]{:S(2)}) collective-permute-start(bf16[48,1152]{1,0:T(8,128)(2,1)S(1)} %get-tuple-element.82), channel_id=1, source_target_pairs={{0,1},{1,0},{2,3},{3,2},{4,5},{5,4},{6,7},{7,6},{8,9},{9,8},{10,11... | collective-permute-start | bytes 331784 | tf_op jit(solution)/shard_map/ppermute | solution.py:597
  128.3 3.4 %collective-permute-done.19.other_ref = bf16[48,1152]{1,0:T(8,128)(2,1)S(1)} collective-permute-done((bf16[48,1152]{1,0:T(8,128)(2,1)S(1)}, bf16[48,1152]{1,0:T(8,128)(2,1)S(1)}, u32[]{:S(2)}, u32[]{:S(2)}) %collective-permute-start.19) | collective-permute-done | bytes 110624 | tf_op jit(solution)/shard_map/ppermute | solution.py:597
  (45 shorter events, 5.7 us)
Async XLA Ops:
  0.0 0.9 copy-start.3
  1.0 9.0 %collective-permute-start.5 = (bf16[48,1152]{1,0:T(8,128)(2,1)S(1)}, bf16[48,1152]{1,0:T(8,128)(2,1)S(1)}, u32[]{:S(2)}, u32[]{:S(2)}) collective-permute-start(bf16[48,1152]{1,0:T(8,128)(2,1)S(1)} %shard_map.130.refs_0_), channel_id=1, source_target_pairs={{4,0},{6,2},{5,1},{7,3},{8,4},{10,6},{9,5},{11,7},{12,8},{14,10},{... | collective-permute-start | bytes 331784 | tf_op jit(solution)/shard_map/ppermute | solution.py:496
  6.5 9.5 %collective-permute-start.7 = (bf16[48,1152]{1,0:T(8,128)(2,1)S(1)}, bf16[48,1152]{1,0:T(8,128)(2,1)S(1)}, u32[]{:S(2)}, u32[]{:S(2)}) collective-permute-start(bf16[48,1152]{1,0:T(8,128)(2,1)S(1)} %shard_map.130.refs_0_), channel_id=1, source_target_pairs={{12,0},{14,2},{13,1},{15,3},{0,4},{2,6},{1,5},{3,7},{4,8},{6,10},{... | collective-permute-start | bytes 331784 | tf_op jit(solution)/shard_map/ppermute | solution.py:496
  6.5 11.1 %collective-permute-start.1 = (bf16[48,1152]{1,0:T(8,128)(2,1)S(1)}, bf16[48,1152]{1,0:T(8,128)(2,1)S(1)}, u32[]{:S(2)}, u32[]{:S(2)}) collective-permute-start(bf16[48,1152]{1,0:T(8,128)(2,1)S(1)} %shard_map.130.refs_0_), channel_id=1, source_target_pairs={{1,0},{3,2},{4,1},{6,3},{5,4},{7,6},{8,5},{10,7},{9,8},{11,10},{12... | collective-permute-start | bytes 331784 | tf_op jit(solution)/shard_map/ppermute | solution.py:496
  7.5 11.0 %collective-permute-start.3 = (bf16[48,1152]{1,0:T(8,128)(2,1)S(1)}, bf16[48,1152]{1,0:T(8,128)(2,1)S(1)}, u32[]{:S(2)}, u32[]{:S(2)}) collective-permute-start(bf16[48,1152]{1,0:T(8,128)(2,1)S(1)} %shard_map.130.refs_0_), channel_id=1, source_target_pairs={{13,0},{15,2},{0,1},{2,3},{1,4},{3,6},{4,5},{6,7},{5,8},{7,10},{8,... | collective-permute-start | bytes 331784 | tf_op jit(solution)/shard_map/ppermute | solution.py:496
  8.5 10.0 %collective-permute-start = (bf16[48,1152]{1,0:T(8,128)(2,1)S(1)}, bf16[48,1152]{1,0:T(8,128)(2,1)S(1)}, u32[]{:S(2)}, u32[]{:S(2)}) collective-permute-start(bf16[48,1152]{1,0:T(8,128)(2,1)S(1)} %shard_map.130.refs_0_), channel_id=1, source_target_pairs={{2,0},{0,2},{3,1},{1,3},{6,4},{4,6},{7,5},{5,7},{10,8},{8,10},{11,... | collective-permute-start | bytes 331784 | tf_op jit(solution)/shard_map/ppermute | solution.py:496
  10.0 9.0 %collective-permute-start.9 = (bf16[48,1152]{1,0:T(8,128)(2,1)S(1)}, bf16[48,1152]{1,0:T(8,128)(2,1)S(1)}, u32[]{:S(2)}, u32[]{:S(2)}) collective-permute-start(bf16[48,1152]{1,0:T(8,128)(2,1)S(1)} %collective-permute-done.5.refs_6_), channel_id=1, source_target_pairs={{1,0},{3,2},{4,1},{6,3},{5,4},{7,6},{8,5},{10,7},{9,8},{11,10},{12... | collective-permute-start | bytes 331784 | tf_op jit(solution)/shard_map/ppermute | solution.py:496
  15.9 6.7 %collective-permute-start.13 = (bf16[48,1152]{1,0:T(8,128)(2,1)S(1)}, bf16[48,1152]{1,0:T(8,128)(2,1)S(1)}, u32[]{:S(2)}, u32[]{:S(2)}) collective-permute-start(bf16[48,1152]{1,0:T(8,128)(2,1)S(1)} %collective-permute-done.5.refs_6_), channel_id=1, source_target_pairs={{4,0},{6,2},{5,1},{7,3},{8,4},{10,6},{9,5},{11,7},{12,8},{14,10},{... | collective-permute-start | bytes 331784 | tf_op jit(solution)/shard_map/ppermute | solution.py:496
  17.5 5.2 %collective-permute-start.11 = (bf16[48,1152]{1,0:T(8,128)(2,1)S(1)}, bf16[48,1152]{1,0:T(8,128)(2,1)S(1)}, u32[]{:S(2)}, u32[]{:S(2)}) collective-permute-start(bf16[48,1152]{1,0:T(8,128)(2,1)S(1)} %collective-permute-done.7.refs_8_), channel_id=1, source_target_pairs={{13,0},{15,2},{0,1},{2,3},{1,4},{3,6},{4,5},{6,7},{5,8},{7,10},{8,... | collective-permute-start | bytes 331784 | tf_op jit(solution)/shard_map/ppermute | solution.py:496
  18.5 4.7 %collective-permute-start.6 = (bf16[48,1152]{1,0:T(8,128)(2,1)S(1)}, bf16[48,1152]{1,0:T(8,128)(2,1)S(1)}, u32[]{:S(2)}, u32[]{:S(2)}) collective-permute-start(bf16[48,1152]{1,0:T(8,128)(2,1)S(1)} %collective-permute-done.5.refs_6_), channel_id=1, source_target_pairs={{2,0},{0,2},{3,1},{1,3},{6,4},{4,6},{7,5},{5,7},{10,8},{8,10},{11,... | collective-permute-start | bytes 331784 | tf_op jit(solution)/shard_map/ppermute | solution.py:496
  18.5 4.8 %collective-permute-start.8 = (bf16[48,1152]{1,0:T(8,128)(2,1)S(1)}, bf16[48,1152]{1,0:T(8,128)(2,1)S(1)}, u32[]{:S(2)}, u32[]{:S(2)}) collective-permute-start(bf16[48,1152]{1,0:T(8,128)(2,1)S(1)} %collective-permute-done.7.refs_8_), channel_id=1, source_target_pairs={{2,0},{0,2},{3,1},{1,3},{6,4},{4,6},{7,5},{5,7},{10,8},{8,10},{11,... | collective-permute-start | bytes 331784 | tf_op jit(solution)/shard_map/ppermute | solution.py:496
  19.0 4.7 %collective-permute-start.2 = (bf16[48,1152]{1,0:T(8,128)(2,1)S(1)}, bf16[48,1152]{1,0:T(8,128)(2,1)S(1)}, u32[]{:S(2)}, u32[]{:S(2)}) collective-permute-start(bf16[48,1152]{1,0:T(8,128)(2,1)S(1)} %collective-permute-done.1.refs_2_), channel_id=1, source_target_pairs={{2,0},{0,2},{3,1},{1,3},{6,4},{4,6},{7,5},{5,7},{10,8},{8,10},{11,... | collective-permute-start | bytes 331784 | tf_op jit(solution)/shard_map/ppermute | solution.py:496
  22.7 1.3 collective-permute-start.4
  22.7 1.5 %collective-permute-start.10 = (bf16[48,1152]{1,0:T(8,128)(2,1)S(1)}, bf16[48,1152]{1,0:T(8,128)(2,1)S(1)}, u32[]{:S(2)}, u32[]{:S(2)}) collective-permute-start(bf16[48,1152]{1,0:T(8,128)(2,1)S(1)} %collective-permute-done.9.refs_10_), channel_id=1, source_target_pairs={{2,0},{0,2},{3,1},{1,3},{6,4},{4,6},{7,5},{5,7},{10,8},{8,10},{11,... | collective-permute-start | bytes 331784 | tf_op jit(solution)/shard_map/ppermute | solution.py:496
  23.2 1.3 collective-permute-start.14
  23.3 1.4 %collective-permute-start.12 = (bf16[48,1152]{1,0:T(8,128)(2,1)S(1)}, bf16[48,1152]{1,0:T(8,128)(2,1)S(1)}, u32[]{:S(2)}, u32[]{:S(2)}) collective-permute-start(bf16[48,1152]{1,0:T(8,128)(2,1)S(1)} %collective-permute-done.11.refs_12_), channel_id=1, source_target_pairs={{2,0},{0,2},{3,1},{1,3},{6,4},{4,6},{7,5},{5,7},{10,8},{8,10},{11,... | collective-permute-start | bytes 331784 | tf_op jit(solution)/shard_map/ppermute | solution.py:496
  27.2 43.2 %collective-permute-start.15 = (bf16[5,48,1152]{2,1,0:T(8,128)(2,1)}, bf16[5,48,1152]{2,1,0:T(8,128)(2,1)S(1)}, u32[]{:S(2)}, u32[]{:S(2)}) collective-permute-start(bf16[5,48,1152]{2,1,0:T(8,128)(2,1)} %get-tuple-element.77), channel_id=1, source_target_pairs={{255,0},{254,1},{253,2},{252,3},{251,4},{250,5},{249,6},{248,7},{2... | collective-permute-start | bytes 1658888 | tf_op jit(solution)/shard_map/ppermute | solution.py:536
  34.6 35.8 %collective-permute-start.16 = (bf16[48,1152]{1,0:T(8,128)(2,1)}, bf16[48,1152]{1,0:T(8,128)(2,1)S(1)}, u32[]{:S(2)}, u32[]{:S(2)}) collective-permute-start(bf16[48,1152]{1,0:T(8,128)(2,1)} %get-tuple-element.78), channel_id=1, source_target_pairs={{15,0},{14,1},{13,2},{12,3},{11,4},{10,5},{9,6},{8,7},{7,8},{6,9},... | collective-permute-start | bytes 331784 | tf_op jit(solution)/shard_map/ppermute | solution.py:536
  36.8 33.5 %collective-permute-start.17 = (bf16[24,1152]{1,0:T(8,128)(2,1)}, bf16[24,1152]{1,0:T(8,128)(2,1)S(1)}, u32[]{:S(2)}, u32[]{:S(2)}) collective-permute-start(bf16[24,1152]{1,0:T(8,128)(2,1)} %get-tuple-element.79), channel_id=1, source_target_pairs={{241,0},{240,1},{255,2},{254,3},{253,4},{252,5},{251,6},{250,7},{2... | collective-permute-start | bytes 165896 | tf_op jit(solution)/shard_map/ppermute | solution.py:536
  40.4 29.9 %collective-permute-start.18 = (bf16[8,1152]{1,0:T(8,128)(2,1)}, bf16[8,1152]{1,0:T(8,128)(2,1)S(1)}, u32[]{:S(2)}, u32[]{:S(2)}) collective-permute-start(bf16[8,1152]{1,0:T(8,128)(2,1)} %get-tuple-element.80), channel_id=1, source_target_pairs={{1,0},{0,1},{15,2},{14,3},{13,4},{12,5},{11,6},{10,7},{9,8},{8,9},... | collective-permute-start | bytes 55304 | tf_op jit(solution)/shard_map/ppermute | solution.py:536
  70.3 28.8 %copy-start.2 = (bf16[2,4,128,192]{3,2,1,0:T(8,128)(2,1)S(1)}, bf16[2,4,128,192]{3,2,1,0:T(8,128)(2,1)}, u32[]{:S(2)}) copy-start(bf16[2,4,128,192]{3,2,1,0:T(8,128)(2,1)} %constant.81.clone.table_ref) | copy-start | bytes 1179652
  79.3 45.4 %copy-start = (bf16[1,1024,768]{2,1,0:T(8,128)(2,1)S(1)}, bf16[1,1024,768]{2,1,0:T(8,128)(2,1)}, u32[]{:S(2)}) copy-start(bf16[1,1024,768]{2,1,0:T(8,128)(2,1)} %constant.82.clone.tb_ref) | copy-start | bytes 4718596
  79.3 45.4 %copy-start.1 = (bf16[2,640,384]{2,1,0:T(8,128)(2,1)S(1)}, bf16[2,640,384]{2,1,0:T(8,128)(2,1)}, u32[]{:S(2)}) copy-start(bf16[2,640,384]{2,1,0:T(8,128)(2,1)} %constant.83.clone.ta_ref) | copy-start | bytes 2949124
  126.9 4.8 %collective-permute-start.19 = (bf16[48,1152]{1,0:T(8,128)(2,1)S(1)}, bf16[48,1152]{1,0:T(8,128)(2,1)S(1)}, u32[]{:S(2)}, u32[]{:S(2)}) collective-permute-start(bf16[48,1152]{1,0:T(8,128)(2,1)S(1)} %get-tuple-element.82), channel_id=1, source_target_pairs={{0,1},{1,0},{2,3},{3,2},{4,5},{5,4},{6,7},{7,6},{8,9},{9,8},{10,11... | collective-permute-start | bytes 331784 | tf_op jit(solution)/shard_map/ppermute | solution.py:597
  (4 other events, 2.7 us)
